TPU v7x, 32 devices: a whole 2x2x4 slice. The times are simulated.
32 devices in a mesh: gx: 2 (over x), gy: 4 (over y, core), ch: 4 (over z).
Axes of the slice: x: 2, y: 2, z: 4, core: 2. Of those that a mesh axis runs over, the one named last changes fastest.
Arguments:
- inputs: bfloat16 [8, 16, 32, 256], P('gx', 'gy', None, 'ch'), may hold values from -6 to 6
- weight: bfloat16 [3, 3, 3, 256, 256], P(None, None, None, 'ch'), may hold values from -0.109375 to 0.109375
- bias: bfloat16 [256], P('ch'), may hold values from -3 to 3
- cotangent: bfloat16 [8, 16, 32, 256], P('gx', 'gy', None, 'ch'), may hold values from -6 to 6
Outputs:
- activation: bfloat16 [8, 16, 32, 256], P('gx', 'gy', None, 'ch')
- input_grad: bfloat16 [8, 16, 32, 256], P('gx', 'gy', None, 'ch')
- weight_grad: float32 [3, 3, 3, 256, 256], P(None, None, None, 'ch')
- bias_grad: float32 [256], P('ch')
All inputs are finite; a program needn't handle non-finite values.
Results may differ from a plain program's by a relative error of at most 0.0075.
Values may be sent and summed in bfloat16 or wider, within the bound.
No kernel may reach another device: no remote copies, remote signals or barrier semaphores. Data moves between devices by JAX's collectives and lax.ppermute only.
A program may use at most 64 MiB of HBM per device.

v0:
```python
import functools
import math

import jax
import jax.numpy as jnp
from jax import lax
from jax.experimental import pallas as pl
from jax.experimental.pallas import tpu as pltpu
from jax.sharding import PartitionSpec as P

VMEM = pl.BlockSpec(memory_space=pltpu.VMEM)
HBM = pl.BlockSpec(memory_space=pltpu.HBM)
SMEM = pl.BlockSpec(memory_space=pltpu.SMEM)
PARAMS = pltpu.CompilerParams(vmem_limit_bytes=24 * 1024 * 1024)
F32 = jnp.float32
BF16 = jnp.bfloat16


def with_halo(x, sides, width):
    for axis, dim in sides:
        devices, length = (lax.axis_size(axis), x.shape[dim])
        up = [(i, (i + 1) % devices) for i in range(devices - 1)]
        down = [(j, i) for i, j in up]
        last = lax.slice_in_dim(x, length - width, length, axis=dim)
        initial = lax.slice_in_dim(x, 0, width, axis=dim)
        before = lax.ppermute(last, axis, up)
        after = lax.ppermute(initial, axis, down)
        x = jnp.concatenate([before, x, after], axis=dim)
    return x


def body_reduced(inputs, weight, bias, cotangent):
    span_x, span_y, span_z, local_ch = inputs.shape
    widest = weight.shape[4]
    local_cells = span_x * span_y * span_z
    offsets = [(a, b, c) for a in range(3) for b in range(3) for c in range(3)]
    depth_pad = ((0, 0), (0, 0), (1, 1), (0, 0))
    rimmed = with_halo(inputs, (("gx", 0), ("gy", 1)), 1)
    padded = jnp.pad(rimmed, depth_pad)
    blocks = []
    for a, b, c in offsets:
        blocks.append(
            padded[a : a + span_x, b : b + span_y, c : c + span_z].reshape(local_cells, local_ch)
        )
    patches = jnp.concatenate(blocks, axis=1)
    flat_weight = weight.reshape(27 * local_ch, widest)
    summed = lax.psum_scatter(
        lax.dot_general(flat_weight, patches, (((0,), (1,)), ((), ())), preferred_element_type=F32),
        "ch",
        scatter_dimension=0,
        tiled=True,
    ).T
    summed = summed + bias.astype(F32)[None, :]
    activation = jax.nn.silu(summed).astype(BF16).reshape(span_x, span_y, span_z, local_ch)
    sigmoid_pre = jax.nn.sigmoid(summed)
    slope = (
        cotangent.reshape(local_cells, local_ch).astype(F32)
        * sigmoid_pre
        * (1.0 + summed * (1.0 - sigmoid_pre))
    ).astype(BF16)
    local_bias = jnp.sum(slope.astype(F32), axis=0)
    slope_grid = slope.reshape(span_x, span_y, span_z, local_ch)
    weight_turned = jnp.transpose(weight.reshape(27, local_ch, widest), (0, 2, 1))
    slope_rimmed = with_halo(slope_grid, (("gx", 0), ("gy", 1)), 1)
    piece = lax.all_gather(slope_rimmed, "ch", axis=3, tiled=True)
    extended = jnp.pad(piece, depth_pad)
    running = jnp.zeros((local_cells, local_ch), F32)
    for index, (a, b, c) in enumerate(offsets):
        a, b, c = (2 - a, 2 - b, 2 - c)
        cut = extended[a : a + span_x, b : b + span_y, c : c + span_z].reshape(local_cells, widest)
        running = running + jnp.dot(cut, weight_turned[index], preferred_element_type=F32)
    interior = piece[1 : 1 + span_x, 1 : 1 + span_y].reshape(local_cells, widest)
    product = lax.dot_general(
        patches, interior, (((0,), (0,)), ((), ())), preferred_element_type=F32
    )
    total_cells = local_cells * lax.axis_size("gx") * lax.axis_size("gy")
    factor = 1.0 / math.sqrt(total_cells)
    kernel_total, bias_total = lax.psum((product * factor, local_bias * factor), ("gx", "gy"))
    input_grad = running.astype(BF16).reshape(span_x, span_y, span_z, local_ch)
    return (activation, input_grad, kernel_total.reshape(3, 3, 3, local_ch, widest), bias_total)


def shifted(v, by):
    depth = v.shape[1]
    row = lax.broadcasted_iota(jnp.int32, v.shape, 1)
    if by == 1:
        return jnp.where(row == 0, 0.0, pltpu.roll(v, 1, 1))
    return jnp.where(row == depth - 1, 0.0, pltpu.roll(v, depth - 1, 1))


def rim_sides(place, span_x, span_y):
    first = place[1] % 2 == 0
    even_at = jnp.where(first, span_y + 1, 0)
    odd_at = jnp.where(first, 0, span_y + 1)
    even_row = jnp.where(first, span_y - 1, 0)
    odd_row = jnp.where(first, 0, span_y - 1)
    x_at = jnp.where(place[0] == 0, span_x + 1, 0)
    x_row = jnp.where(place[0] == 0, span_x - 1, 0)
    return even_at, odd_at, even_row, odd_row, x_at, x_row


def prepare_kernel(place, source, inputs, packed, even, odd, even_corner, odd_corner, arrived):
    copy = pltpu.make_async_copy(source, inputs, arrived)
    copy.start()
    copy.wait()
    span_x, span_y, _, _ = inputs.shape
    half = span_x // 2
    _, _, even_row, odd_row, _, x_row = rim_sides(place, span_x, span_y)
    even[...] = inputs[:, even_row]
    odd[...] = inputs[:, odd_row]
    even_corner[...] = inputs[x_row, even_row]
    odd_corner[...] = inputs[x_row, odd_row]
    packed[...] = jnp.concatenate([inputs[:half], inputs[half:]], axis=3)


def stage_kernel(after, *rest):
    count = (len(rest) - 1) // 2
    sources, targets, arrived = rest[:count], rest[count : 2 * count], rest[-1]
    copies = []
    for source, target in zip(sources, targets):
        parts = source.shape[0] if len(source.shape) == 3 else 1
        for n in range(parts):
            here = pl.ds(n, 1) if parts > 1 else slice(None)
            copies.append(
                pltpu.make_async_copy(source.at[here], target.at[here], arrived.at[len(copies)])
            )
    for copy in copies:
        copy.start()
    for copy in copies:
        copy.wait()


def forward_kernel(
    parts_y, place, weight, inputs, packed, even, odd, beside, even_corner, odd_corner, own, *rest
):
    *others, pair, window, blocks = rest
    span_x, span_y, span_z, lanes = inputs.shape
    half_x = span_x // 2
    half = half_x * span_y * span_z
    even_at, odd_at, _, _, x_at, _ = rim_sides(place, span_x, span_y)

    def spread(v):
        flat = v.astype(F32).reshape(-1, span_z, lanes)
        joined = jnp.concatenate([shifted(flat, 1), flat, shifted(flat, -1)], axis=2)
        return joined.astype(BF16).reshape(v.shape[:-1] + (3 * lanes,))

    nothing = jnp.zeros((span_y + 2, span_z, 3 * lanes), BF16)
    window[0] = nothing
    window[span_x + 1] = nothing
    window[1 : span_x + 1, 1 : span_y + 1] = spread(inputs[...])
    window[1 : span_x + 1, even_at] = spread(even[...])
    has_odd = (place[1] != 0) & (place[1] != parts_y - 1)
    window[1 : span_x + 1, odd_at] = jnp.where(has_odd, spread(odd[...]), jnp.zeros((), BF16))
    across = jnp.where(place[0] == 0, beside[0][..., :lanes], beside[half_x - 1][..., lanes:])
    window[x_at, 1 : span_y + 1] = spread(across)
    window[x_at, even_at] = spread(even_corner[...])
    window[x_at, odd_at] = jnp.where(has_odd, spread(odd_corner[...]), jnp.zeros((), BF16))
    sums = []
    for h in range(2):
        total = None
        for a in range(3):
            for b in range(3):
                cut = window[a + h * half_x : a + (h + 1) * half_x, b : b + span_y]
                term = jnp.dot(
                    cut.reshape(half, 3 * lanes), weight[a * 3 + b], preferred_element_type=F32
                )
                total = term if total is None else total + term
        sums.append(total)
    for d in range(weight.shape[2] // lanes):
        cut = slice(d * lanes, (d + 1) * lanes)
        blocks[d] = jnp.concatenate([sums[0][:, cut], sums[1][:, cut]], axis=1)
    own[...] = blocks[place[2]]
    for k, other in enumerate(others):
        other[...] = blocks[place[2] ^ (k + 1)].astype(BF16)
    pair[0] = packed[...]
    pair[1] = beside[...]


def slope_kernel(own, *rest):
    *others, bias, cotangent, active, slope = rest
    half = cotangent.shape[0] // 2
    summed = own[...]
    for other in others:
        summed = summed + other[...].astype(F32)
    offset = bias[...].astype(F32)
    summed = summed + jnp.concatenate([offset, offset], axis=1)
    sigmoid = jax.nn.sigmoid(summed)
    active[...] = (summed * sigmoid).astype(BF16)
    upstream = jnp.concatenate([cotangent[:half], cotangent[half:]], axis=1).astype(F32)
    slope[...] = (upstream * sigmoid * (1.0 + summed * (1.0 - sigmoid))).astype(BF16)


def ordered_halves(place, pieces):
    shards, _, _, _, lanes = pieces.shape
    lanes = lanes // 2
    ordered = [pieces[place[2] ^ j] for j in range(shards)]
    return [
        jnp.concatenate([piece[..., h * lanes : (h + 1) * lanes] for piece in ordered], axis=-1)
        for h in range(2)
    ]


def add_terms(place, parts_y, members, slopes, turned, old, store):
    operands = []
    for m, pieces in zip(members, slopes):
        shards, half_x, span_y, span_z, lanes = pieces.shape
        channels, row = shards * lanes // 2, span_y * span_z
        right = jnp.concatenate(
            [part.reshape(half_x * row, channels) for part in ordered_halves(place, pieces)]
        )
        x0, y0 = (place[0] ^ (m // parts_y)) * 2 * half_x, place[1] ^ (m % parts_y)
        operands.append((x0, y0, row, right))
    for a in range(3):
        total = None if old is None else old[a]
        for x0, y0, row, right in operands:
            left = turned[y0, :, pl.ds(pl.multiple_of((x0 + a) * row, row), right.shape[0])]
            term = jnp.dot(left, right, preferred_element_type=F32)
            total = term if total is None else total + term
        store(a, total)


def first_kernel(parts_x, parts_y, place, weight, active, pair, beside_y, sibling, column, *rest):
    activation, turned, sums, weight_turned, volume, unpacked, sent = rest
    half, lanes = active.shape[0], active.shape[1] // 2
    unpacked[:half] = active[:, :lanes]
    unpacked[half:] = active[:, lanes:]
    copy = pltpu.make_async_copy(unpacked, activation, sent)
    copy.start()
    shards, half_x, span_y, span_z, lanes = column.shape
    cells = [(0, pair, 0), (parts_y, pair, 1), (2, beside_y, 1), (parts_y + 2, beside_y, 2)]
    cells += [(m ^ 1, sibling, shards + n) for n, (m, _, _) in enumerate(cells)]
    span_x, lanes = 2 * half_x, lanes // 2
    rows_x, rows_y = parts_x * span_x, parts_y * span_y
    width = 3 * lanes
    zero_x = jnp.zeros((1, rows_y + 2, span_z, width), BF16)
    zero_y = jnp.zeros((rows_x + 2, 1, span_z, width), BF16)
    volume[0:1] = zero_x
    volume[rows_x + 1 : rows_x + 2] = zero_x
    volume[:, 0:1] = zero_y
    volume[:, rows_y + 1 : rows_y + 2] = zero_y
    for m, array, n in cells:
        x0, y0 = (place[0] ^ (m // parts_y)) * span_x, (place[1] ^ (m % parts_y)) * span_y
        v = array[n].astype(F32).reshape(half_x * span_y, span_z, 2 * lanes)
        low, high = shifted(v, 1), shifted(v, -1)
        for h in range(2):
            cut = slice(h * lanes, (h + 1) * lanes)
            joined = jnp.concatenate([low[..., cut], v[..., cut], high[..., cut]], axis=2)
            volume[pl.ds(x0 + 1 + h * half_x, half_x), pl.ds(y0 + 1, span_y)] = joined.astype(
                BF16
            ).reshape(half_x, span_y, span_z, width)
    for y in range(parts_y):
        for b in range(3):
            cut = volume[:, y * span_y + b : (y + 1) * span_y + b]
            turned[y, b * width : (b + 1) * width] = cut.reshape(-1, width).T

    def store(a, total):
        sums[a] = total

    for tap in range(weight.shape[0]):
        weight_turned[tap] = weight[tap].T
    members = (0, 1)
    add_terms(place, parts_y, members, (column, sibling.at[:shards]), turned, None, store)
    copy.wait()


def rows_of(place, pieces, row):
    shards, lanes = column_shape(pieces)
    ordered = [pieces[place[2] ^ j, :, row] for j in range(shards)]
    return [
        jnp.concatenate([piece[..., h * lanes : (h + 1) * lanes] for piece in ordered], axis=-1)
        for h in range(2)
    ]


def column_shape(pieces):
    return pieces.shape[0], pieces.shape[-1] // 2


def second_kernel(
    parts_y, members, place, weight, turned, old, column, sibling, *rest
):
    *slopes, partial, sums, window = rest
    shards, half_x, span_y, span_z, _ = column.shape
    span_x, half = 2 * half_x, half_x * span_y * span_z
    even_at, _, even_row, _, _, _ = rim_sides(place, span_x, span_y)
    window[...] = jnp.zeros(window.shape, BF16)
    beside = rows_of(place, sibling.at[:shards], facing_row(even_row, span_y))
    for h, own in enumerate(ordered_halves(place, column)):
        window[1 + h * half_x : 1 + (h + 1) * half_x, 1 : span_y + 1] = own
        window[1 + h * half_x : 1 + (h + 1) * half_x, even_at] = beside[h]
    for h in range(2):
        total = None
        for a in range(3):
            for b in range(3):
                cut = window[
                    2 - a + h * half_x : 2 - a + (h + 1) * half_x, 2 - b : 2 - b + span_y
                ]
                term = jnp.dot(
                    cut.reshape(half, cut.shape[-1]), weight[a * 3 + b], preferred_element_type=F32
                )
                total = term if total is None else total + term
        partial[h * half_x : (h + 1) * half_x] = total.reshape((half_x,) + partial.shape[1:])
    middle_kernel(parts_y, members, place, turned, old, *slopes, sums)


def middle_kernel(parts_y, members, place, turned, old, *rest):
    *slopes, sums = rest

    def store(a, total):
        sums[a] = total

    add_terms(place, parts_y, members, slopes, turned, old, store)


def facing(place, halves):
    low, high = halves
    return jnp.where(place[0] == 0, low[0], high[-1])


def channel_sum(pieces):
    mine = pieces[0].astype(F32).reshape(-1, pieces.shape[-1])
    return jnp.sum(mine, axis=0, keepdims=True)


def rim_kernel(parts_y, members, place, weight, turned, old, partial, *rest):
    *slopes, grid, column, sums, rim_x, rim_y = rest
    shards, half_x, span_y, span_z, _ = slopes[0].shape
    span_x, channels = 2 * half_x, rim_x.shape[-1]
    even_at, odd_at, even_row, odd_row, _, x_row = rim_sides(place, span_x, span_y)
    has_odd = (place[1] != 0) & (place[1] != parts_y - 1)
    rim_x[...] = jnp.zeros(rim_x.shape, BF16)
    rim_y[...] = jnp.zeros(rim_y.shape, BF16)
    rim_x[1 : span_y + 1] = facing(place, ordered_halves(place, slopes[parts_y]))
    even = rows_of(place, slopes[parts_y + 1], facing_row(even_row, span_y))
    rim_x[even_at] = facing(place, even)

    @pl.when(has_odd)
    def _():
        odd = rows_of(place, slopes[3], facing_row(odd_row, span_y))
        for h, rows in enumerate(odd):
            rim_y[1 + h * half_x : 1 + (h + 1) * half_x] = rows

    grid[...] = partial[...]
    tap_x, tap_y = rim_taps(place, odd_row)
    total = None
    for b in range(3):
        cut = rim_x[2 - b : 2 - b + span_y].reshape(span_y * span_z, channels)
        term = jnp.dot(cut, weight[tap_x * 3 + b], preferred_element_type=F32)
        total = term if total is None else total + term
    grid[x_row] += total.reshape((span_y,) + grid.shape[2:])
    total = None
    for a in range(3):
        cut = rim_y[2 - a : 2 - a + span_x].reshape(span_x * span_z, channels)
        term = jnp.dot(cut, weight[a * 3 + tap_y], preferred_element_type=F32)
        total = term if total is None else total + term
    grid[:, odd_row] += total.reshape((span_x,) + grid.shape[2:])
    total = channel_sum(slopes[0])
    for pieces in slopes[1:]:
        total = total + channel_sum(pieces)
    column[...] = total
    middle_kernel(parts_y, members, place, turned, old, *[slopes[m] for m in members], sums)


def rim_taps(place, odd_row):
    return jnp.where(place[0] == 0, 0, 2), jnp.where(odd_row == 0, 2, 0)


def last_kernel(parts_y, member, factor, place, weight, turned, old, partial, column, pieces, *rest):
    input_grad, kernel_grad, bias_grad, grid, sums, cells, bias, sent = rest
    _, half_x, span_y, span_z, _ = pieces.shape
    lanes = pieces.shape[-1] // 2
    span_x = 2 * half_x
    copies = []

    def send(source, target):
        copies.append(pltpu.make_async_copy(source, target, sent.at[len(copies)]))
        copies[-1].start()

    def store(a, total):
        sums[a] = total * factor
        send(sums.at[a], kernel_grad.at[a])

    add_terms(place, parts_y, (member,), (pieces,), turned, old, store)

    _, _, _, odd_row, _, x_row = rim_sides(place, span_x, span_y)
    has_odd = (place[1] != 0) & (place[1] != parts_y - 1)
    tap_x, tap_y = rim_taps(place, odd_row)
    grid[...] = partial[...]

    @pl.when(has_odd)
    def _():
        corner = facing(place, rows_of(place, pieces, facing_row(odd_row, span_y)))
        term = jnp.dot(corner, weight[tap_x * 3 + tap_y], preferred_element_type=F32)
        grid[x_row, odd_row] += term

    summed = grid[...].reshape(span_x * span_y, span_z, 3 * lanes)
    result = (
        shifted(summed[..., :lanes], -1)
        + summed[..., lanes : 2 * lanes]
        + shifted(summed[..., 2 * lanes :], 1)
    )
    cells[...] = result.reshape(-1, lanes).astype(BF16)
    send(cells, input_grad)
    total = column[...] + channel_sum(pieces)
    bias[...] = (total[:, :lanes] + total[:, lanes:]) * factor
    send(bias, bias_grad)
    for copy in copies:
        copy.wait()


def facing_row(row, span_y):
    return span_y - 1 - row


def exchange(x, axes, mask):
    return lax.ppermute(x, axes, [(i, i ^ mask) for i in range(lax.axis_size(axes))])


def body_gathered(inputs, weight, bias, cotangent):
    spans = inputs.shape[:3]
    span_x, span_y, span_z = spans
    local_ch, channels = weight.shape[3:]
    local = span_x * span_y * span_z
    parts_x, parts_y = lax.axis_size("gx"), lax.axis_size("gy")
    count = parts_x * parts_y
    shards = lax.axis_size("ch")
    axes = ("gx", "gy")
    factor = 1.0 / math.sqrt(local * count)
    place = jnp.stack([lax.axis_index(axis) for axis in ("gx", "gy", "ch")]).astype(jnp.int32)
    taps = weight.reshape(9, 3 * local_ch, channels)
    packing = (span_x // 2, span_y, span_z, 2 * local_ch)
    flat = (local // 2, 2 * local_ch)

    def call(kernel, name, outs, args, scratch=()):
        return pl.pallas_call(
            kernel,
            out_shape=[jax.ShapeDtypeStruct(shape, kind) for shape, kind in outs],
            in_specs=[SMEM if x is place else VMEM for x in args],
            out_specs=[VMEM] * len(outs),
            scratch_shapes=[pltpu.VMEM(shape, kind) for shape, kind in scratch],
            compiler_params=PARAMS,
            cost_estimate=pl.CostEstimate(flops=0, bytes_accessed=1024, transcendentals=0),
            name=name,
        )(*args)

    row = (span_x, span_z, local_ch)
    held, packed, even, odd, even_corner, odd_corner = pl.pallas_call(
        prepare_kernel,
        out_shape=[jax.ShapeDtypeStruct(inputs.shape, BF16), jax.ShapeDtypeStruct(packing, BF16)]
        + [jax.ShapeDtypeStruct(row, BF16)] * 2
        + [jax.ShapeDtypeStruct(row[1:], BF16)] * 2,
        in_specs=[SMEM, HBM],
        out_specs=[VMEM] * 6,
        scratch_shapes=[pltpu.SemaphoreType.DMA],
        compiler_params=PARAMS,
        name="prepare",
    )(place, pltpu.with_memory_space_constraint(inputs, pltpu.HBM))
    sources = (taps, cotangent.reshape(local, local_ch), bias.reshape(1, local_ch))
    taps, cotangent, bias = pl.pallas_call(
        stage_kernel,
        out_shape=[jax.ShapeDtypeStruct(x.shape, x.dtype) for x in sources],
        in_specs=[VMEM] + [HBM] * len(sources),
        out_specs=[VMEM] * len(sources),
        scratch_shapes=[pltpu.SemaphoreType.DMA((len(sources) + 8,))],
        compiler_params=PARAMS,
        name="stage",
    )(even_corner, *[pltpu.with_memory_space_constraint(x, pltpu.HBM) for x in sources])
    beside = exchange(packed, axes, parts_y)
    even = exchange(even, axes, 1)
    odd = exchange(odd, axes, 3)
    even_corner = exchange(even_corner, axes, parts_y + 1)
    odd_corner = exchange(odd_corner, axes, parts_y + 3)
    own, *others, pair = call(
        functools.partial(forward_kernel, parts_y),
        "forward",
        [(flat, F32)] + [(flat, BF16)] * (shards - 1) + [((2,) + packing, BF16)],
        [place, taps, held, packed, even, odd, beside, even_corner, odd_corner],
        [((span_x + 2, span_y + 2, span_z, 3 * local_ch), BF16), ((shards,) + flat, F32)],
    )
    others = [exchange(others[k - 1], "ch", k) for k in range(shards - 1, 0, -1)]
    active, slope = call(
        slope_kernel,
        "slope",
        [(flat, BF16), (flat, BF16)],
        [own, *others, bias, cotangent],
    )
    rest = [exchange(slope, "ch", k) for k in range(1, shards)]
    rest = jnp.stack(rest).reshape((shards - 1,) + packing)
    piece = slope.reshape((1,) + packing)
    x, y = parts_y, 2
    beside_x = exchange(piece, axes, x)
    beside_y = exchange(jnp.concatenate([piece, pair]), axes, y)
    beside_y, beside_x, rest = lax.optimization_barrier((beside_y, beside_x, rest))
    column = jnp.concatenate([piece, rest])
    late_y, late_x = exchange(rest, axes, y), exchange(rest, axes, x)
    sibling = exchange(jnp.concatenate([column, pair, beside_y[1:]]), axes, 1)
    turned_shape = (parts_y, 9 * local_ch, (parts_x * span_x + 2) * span_y * span_z)
    sums_shape = (3, 9 * local_ch, channels)
    first_outs = [((local, local_ch), BF16), (turned_shape, BF16), (sums_shape, F32)]
    first_outs += [((9, channels, 3 * local_ch), BF16)]
    args = [place, taps, active, pair, beside_y, sibling, column]
    activation, turned, sums, taps = pl.pallas_call(
        functools.partial(first_kernel, parts_x, parts_y),
        out_shape=[jax.ShapeDtypeStruct(shape, kind) for shape, kind in first_outs],
        in_specs=[SMEM] + [VMEM] * (len(args) - 1),
        out_specs=[HBM] + [VMEM] * 3,
        scratch_shapes=[
            pltpu.VMEM((parts_x * span_x + 2, parts_y * span_y + 2, span_z, 3 * local_ch), BF16),
            pltpu.VMEM((local, local_ch), BF16),
            pltpu.SemaphoreType.DMA,
        ],
        compiler_params=PARAMS,
        cost_estimate=pl.CostEstimate(flops=0, bytes_accessed=1024, transcendentals=0),
        name="first",
    )(*args)
    slopes = {0: column, 1: sibling[:shards]}
    late_y, late_x, sums = lax.optimization_barrier((late_y, late_x, sums))
    slopes[y] = jnp.concatenate([beside_y[:1], late_y])
    slopes[x] = jnp.concatenate([beside_x, late_x])
    middle = shards // 2
    diagonal = [exchange(slopes[x][:middle], axes, y), exchange(slopes[y][middle:], axes, x)]
    across = [exchange(slopes[m], axes, 1) for m in (y, x)]
    grid_shape = spans + (3 * local_ch,)
    partial, sums = call(
        functools.partial(second_kernel, parts_y, (y, x)),
        "second",
        [(grid_shape, F32), (sums_shape, F32)],
        [place, taps, turned, sums, column, sibling, slopes[y], slopes[x]],
        [((span_x + 2, span_y + 2, span_z, channels), BF16)],
    )
    slopes[y + 1], slopes[x + 1] = across
    (sums,) = call(
        functools.partial(middle_kernel, parts_y, (y + 1, x + 1)),
        "third",
        [(sums_shape, F32)],
        [place, turned, sums, *across],
    )
    *diagonal, sums = lax.optimization_barrier((*diagonal, sums))
    slopes[x + y] = jnp.concatenate(diagonal)
    final = exchange(slopes[x + y], axes, 1)
    partial, column, sums = call(
        functools.partial(rim_kernel, parts_y, (x + y,)),
        "rim",
        [(grid_shape, F32), ((1, 2 * local_ch), F32), (sums_shape, F32)],
        [place, taps, turned, sums, partial] + [slopes[m] for m in range(count - 1)],
        [((span_y + 2, span_z, channels), BF16), ((span_x + 2, span_z, channels), BF16)],
    )
    args = [place, taps, turned, sums, partial, column, final]
    input_grad, kernel_grad, bias_grad = pl.pallas_call(
        functools.partial(last_kernel, parts_y, x + y + 1, factor),
        out_shape=[
            jax.ShapeDtypeStruct((local, local_ch), BF16),
            jax.ShapeDtypeStruct(sums_shape, F32),
            jax.ShapeDtypeStruct((1, local_ch), F32),
        ],
        in_specs=[SMEM] + [VMEM] * (len(args) - 1),
        out_specs=[HBM] * 3,
        scratch_shapes=[
            pltpu.VMEM(grid_shape, F32),
            pltpu.VMEM(sums_shape, F32),
            pltpu.VMEM((local, local_ch), BF16),
            pltpu.VMEM((1, local_ch), F32),
            pltpu.SemaphoreType.DMA((5,)),
        ],
        compiler_params=PARAMS,
        name="last",
    )(*args)
    return (
        activation.reshape(inputs.shape),
        input_grad.reshape(inputs.shape),
        kernel_grad.reshape(weight.shape),
        bias_grad.reshape(local_ch),
    )


def solution(mesh):
    few = (mesh.shape["gx"], mesh.shape["gy"]) == (2, 4)
    return jax.shard_map(
        body_gathered if few else body_reduced,
        mesh=mesh,
        in_specs=(
            P("gx", "gy", None, "ch"),
            P(None, None, None, "ch", None),
            P("ch"),
            P("gx", "gy", None, "ch"),
        ),
        out_specs=(
            P("gx", "gy", None, "ch"),
            P("gx", "gy", None, "ch"),
            P(None, None, None, "ch", None),
            P("ch"),
        ),
        check_vma=False,
    )
```

profile of v0, /device:TPU:1, one launch (start us, length us, event | category | flops | bytes accessed | tf_op | source)
XLA Modules:
  0.0 51.5 jit_solution(11907392368781937178)
XLA Ops:
  0.7 1.5 %prepare.1 = (bf16[4,4,32,64]{3,2,1,0:T(8,128)(2,1)S(1)}, bf16[2,4,32,128]{3,2,1,0:T(8,128)(2,1)S(1)}, bf16[4,32,64]{2,1,0:T(8,128)(2,1)S(1)}, bf16[4,32,64]{2,1...) custom-call(s32[3]{0:T(128)S(1)} %pad_add_fusion.place, bf16[4,4,32,64]{3,2,1,0:T(8,128)(2,1)} %source.1), custom_call_target="tpu_custom_call" | custom-call | tf_op jit(solution)/shard_map/prepare/pallas_call | solution.py:447
  2.3 2.1 %collective-permute-start.2 = (bf16[2,4,32,128]{3,2,1,0:T(8,128)(2,1)S(1)}, bf16[2,4,32,128]{3,2,1,0:T(8,128)(2,1)S(1)}, u32[]{:S(2)}, u32[]{:S(2)}) collective-permute-start(bf16[2,4,32,128]{3,2,1,0:T(8,128)(2,1)S(1)} %get-tuple-element.44.packed), channel_id=1, source_target_pairs={{0,16},{4,20},{8,24},{12,28},{16,0},{20,4},{24,8},{28,12},{1,17},{... | collective-permute-start | bytes 196616 | tf_op jit(solution)/shard_map/ppermute | solution.py:416
  4.4 1.0 %collective-permute-start = (bf16[4,32,64]{2,1,0:T(8,128)(2,1)S(1)}, bf16[4,32,64]{2,1,0:T(8,128)(2,1)S(1)}, u32[]{:S(2)}, u32[]{:S(2)}) collective-permute-start(bf16[4,32,64]{2,1,0:T(8,128)(2,1)S(1)} %get-tuple-element.45), channel_id=1, source_target_pairs={{0,4},{4,0},{8,12},{12,8},{16,20},{20,16},{24,28},{28,24},{1,5},{5... | collective-permute-start | bytes 49160 | tf_op jit(solution)/shard_map/ppermute | solution.py:416
  5.3 1.1 %collective-permute-start.1 = (bf16[4,32,64]{2,1,0:T(8,128)(2,1)S(1)}, bf16[4,32,64]{2,1,0:T(8,128)(2,1)S(1)}, u32[]{:S(2)}, u32[]{:S(2)}) collective-permute-start(bf16[4,32,64]{2,1,0:T(8,128)(2,1)S(1)} %get-tuple-element.46), channel_id=1, source_target_pairs={{0,12},{4,8},{8,4},{12,0},{16,28},{20,24},{24,20},{28,16},{1,13},{... | collective-permute-start | bytes 49160 | tf_op jit(solution)/shard_map/ppermute | solution.py:416
  6.4 0.1 collective-permute-start.4
  6.6 1.5 %collective-permute-start.3 = (bf16[32,64]{1,0:T(8,128)(2,1)S(1)}, bf16[32,64]{1,0:T(8,128)(2,1)S(1)}, u32[]{:S(2)}, u32[]{:S(2)}) collective-permute-start(bf16[32,64]{1,0:T(8,128)(2,1)S(1)} %get-tuple-element.41.after), channel_id=1, source_target_pairs={{0,20},{4,16},{8,28},{12,24},{16,4},{20,0},{24,12},{28,8},{1,21},{... | collective-permute-start | bytes 12296 | tf_op jit(solution)/shard_map/ppermute | solution.py:416
  8.1 1.4 %stage.1 = (bf16[9,192,256]{2,1,0:T(8,128)(2,1)S(1)}, bf16[512,64]{1,0:T(8,128)(2,1)S(1)}, bf16[1,64]{1,0:T(2,128)(2,1)S(1)}) custom-call(bf16[32,64]{1,0:T(8,128)(2,1)S(1)} %get-tuple-element.41.after, bf16[9,192,256]{2,1,0:T(8,128)(2,1)} %bitcast.18, bf16[512,64]{1,0:T(8,128)(2,1)} %bitcast.19, bf16[1,64]{1,0:T(2,128)(2,1)} %bitcast.23), custom_call_target="tpu_custom_call" | custom-call | tf_op jit(solution)/shard_map/stage/pallas_call | solution.py:459
  9.5 1.0 %collective-permute-done.4.odd_corner = bf16[32,64]{1,0:T(8,128)(2,1)S(1)} collective-permute-done((bf16[32,64]{1,0:T(8,128)(2,1)S(1)}, bf16[32,64]{1,0:T(8,128)(2,1)S(1)}, u32[]{:S(2)}, u32[]{:S(2)}) %collective-permute-start.4) | collective-permute-done | bytes 4128 | tf_op jit(solution)/shard_map/ppermute | solution.py:416
  10.6 1.6 %forward.1 = (f32[256,128]{1,0:T(8,128)S(1)}, bf16[256,128]{1,0:T(8,128)(2,1)S(1)}, bf16[256,128]{1,0:T(8,128)(2,1)S(1)}, bf16[256,128]{1,0:T(8,128)(2,1)S(1)}, bf16[2,2,4,32,128]{4,3,2,1,0:T(8,128)(2,1)S(1)}) custom-call(s32[3]{0:T(128)S(1)} %pad_add_fusion.place, bf16[9,192,256]{2,1,0:T(8,128)(2,1)S(1)} %get-tuple-element.42.weight, ...), custom_call_target="tpu_custom_call" | custom-call | bytes 1024 | tf_op jit(solution)/shard_map/forward/pallas_call | solution.py:435
  12.2 3.4 %collective-permute-start.5 = (bf16[256,128]{1,0:T(8,128)(2,1)S(1)}, bf16[256,128]{1,0:T(8,128)(2,1)S(1)}, u32[]{:S(2)}, u32[]{:S(2)}) collective-permute-start(bf16[256,128]{1,0:T(8,128)(2,1)S(1)} %get-tuple-element.49), channel_id=1, source_target_pairs={{0,3},{1,2},{2,1},{3,0},{4,7},{5,6},{6,5},{7,4},{8,11},{9,10},{10,... | collective-permute-start | bytes 196616 | tf_op jit(solution)/shard_map/ppermute | solution.py:416
  15.6 0.4 collective-permute-start.7
  15.9 1.4 %collective-permute-done.5.rest_0_ = bf16[256,128]{1,0:T(8,128)(2,1)S(1)} collective-permute-done((bf16[256,128]{1,0:T(8,128)(2,1)S(1)}, bf16[256,128]{1,0:T(8,128)(2,1)S(1)}, u32[]{:S(2)}, u32[]{:S(2)}) %collective-permute-start.5) | collective-permute-done | bytes 65568 | tf_op jit(solution)/shard_map/ppermute | solution.py:416
  17.3 4.0 %collective-permute-done.6.rest_1_ = bf16[256,128]{1,0:T(8,128)(2,1)S(1)} collective-permute-done((bf16[256,128]{1,0:T(8,128)(2,1)S(1)}, bf16[256,128]{1,0:T(8,128)(2,1)S(1)}, u32[]{:S(2)}, u32[]{:S(2)}) %collective-permute-start.6) | collective-permute-done | bytes 65568 | tf_op jit(solution)/shard_map/ppermute | solution.py:416
  21.3 0.1 slope.1
  21.5 0.7 %collective-permute-start.8 = (bf16[3,2,4,32,128]{4,3,2,1,0:T(8,128)(2,1)S(1)}, bf16[3,2,4,32,128]{4,3,2,1,0:T(8,128)(2,1)S(1)}, u32[]{:S(2)}, u32[]{:S(2)}) collective-permute-start(bf16[3,2,4,32,128]{4,3,2,1,0:T(8,128)(2,1)S(1)} %pad_maximum_fusion.3), channel_id=1, source_target_pairs={{0,8},{4,12},{8,0},{12,4},{16,24},{20,28},{24,16},{28,20},{1,9},{5... | collective-permute-start | bytes 589832 | tf_op jit(solution)/shard_map/ppermute | solution.py:416
  22.2 2.3 %collective-permute-start.12 = (bf16[256,128]{1,0:T(8,128)(2,1)S(1)}, bf16[256,128]{1,0:T(8,128)(2,1)S(1)}, u32[]{:S(2)}, u32[]{:S(2)}) collective-permute-start(bf16[256,128]{1,0:T(8,128)(2,1)S(1)} %get-tuple-element.56), channel_id=1, source_target_pairs={{0,3},{1,2},{2,1},{3,0},{4,7},{5,6},{6,5},{7,4},{8,11},{9,10},{10,... | collective-permute-start | bytes 196616 | tf_op jit(solution)/shard_map/ppermute | solution.py:416
  24.5 1.3 %collective-permute-start.10 = (bf16[256,128]{1,0:T(8,128)(2,1)S(1)}, bf16[256,128]{1,0:T(8,128)(2,1)S(1)}, u32[]{:S(2)}, u32[]{:S(2)}) collective-permute-start(bf16[256,128]{1,0:T(8,128)(2,1)S(1)} %get-tuple-element.56), channel_id=1, source_target_pairs={{0,1},{1,0},{2,3},{3,2},{4,5},{5,4},{6,7},{7,6},{8,9},{9,8},{10,11... | collective-permute-start | bytes 196616 | tf_op jit(solution)/shard_map/ppermute | solution.py:416
  25.8 1.3 %collective-permute-start.9 = (bf16[1,2,4,32,128]{4,3,2,1,0:T(8,128)(2,1)S(1)}, bf16[1,2,4,32,128]{4,3,2,1,0:T(8,128)(2,1)S(1)}, u32[]{:S(2)}, u32[]{:S(2)}) collective-permute-start(bf16[1,2,4,32,128]{4,3,2,1,0:T(8,128)(2,1)S(1)} %bitcast.15), channel_id=1, source_target_pairs={{0,16},{4,20},{8,24},{12,28},{16,0},{20,4},{24,8},{28,12},{1,17},{... | collective-permute-start | bytes 196616 | tf_op jit(solution)/shard_map/ppermute | solution.py:416
  27.1 3.9 %collective-permute-done.11 = bf16[256,128]{1,0:T(8,128)(2,1)S(1)} collective-permute-done((bf16[256,128]{1,0:T(8,128)(2,1)S(1)}, bf16[256,128]{1,0:T(8,128)(2,1)S(1)}, u32[]{:S(2)}, u32[]{:S(2)}) %collective-permute-start.11) | collective-permute-done | bytes 65568 | tf_op jit(solution)/shard_map/ppermute | solution.py:416
  31.2 1.1 %collective-permute-start.13 = (bf16[8,2,4,32,128]{4,3,2,1,0:T(8,128)(2,1)S(1)}, bf16[8,2,4,32,128]{4,3,2,1,0:T(8,128)(2,1)S(1)}, u32[]{:S(2)}, u32[]{:S(2)}) collective-permute-start(bf16[8,2,4,32,128]{4,3,2,1,0:T(8,128)(2,1)S(1)} %pad_maximum_fusion), channel_id=1, source_target_pairs={{0,4},{4,0},{8,12},{12,8},{16,20},{20,16},{24,28},{28,24},{1,5},{5... | collective-permute-start | bytes 1572872 | tf_op jit(solution)/shard_map/ppermute | solution.py:416
  32.2 1.3 %collective-permute-start.15 = (bf16[3,2,4,32,128]{4,3,2,1,0:T(8,128)(2,1)S(1)}, bf16[3,2,4,32,128]{4,3,2,1,0:T(8,128)(2,1)S(1)}, u32[]{:S(2)}, u32[]{:S(2)}) collective-permute-start(bf16[3,2,4,32,128]{4,3,2,1,0:T(8,128)(2,1)S(1)} %pad_maximum_fusion.4), channel_id=1, source_target_pairs={{0,16},{4,20},{8,24},{12,28},{16,0},{20,4},{24,8},{28,12},{1,17},{... | collective-permute-start | bytes 589832 | tf_op jit(solution)/shard_map/ppermute | solution.py:416
  33.5 0.2 collective-permute-start.14
  33.8 5.0 %first.1 = (bf16[512,64]{1,0:T(8,128)(2,1)}, bf16[4,576,1280]{2,1,0:T(8,128)(2,1)S(1)}, f32[3,576,256]{2,1,0:T(8,128)S(1)}, bf16[9,256,192]{2,1,0:T(8,128)(2,1)S(1)}) custom-call(s32[3]{0:T(128)S(1)} %pad_add_fusion.place, bf16[9,192,256]{2,1,0:T(8,128)(2,1)S(1)} %get-tuple-element.42.weight, bf16[256,128]{1,0:T(8,128)(2,1)S(1)} %get-tuple-element.54.active, ...), custom_call_target="tpu_custom_call" | custom-call | bytes 1024 | tf_op jit(solution)/shard_map/first/pallas_call | solution.py:502
  38.8 0.8 %collective-permute-done.14 = bf16[3,2,4,32,128]{4,3,2,1,0:T(8,128)(2,1)S(1)} collective-permute-done((bf16[3,2,4,32,128]{4,3,2,1,0:T(8,128)(2,1)S(1)}, bf16[3,2,4,32,128]{4,3,2,1,0:T(8,128)(2,1)S(1)}, u32[]{:S(2)}, u32[]{:S(2)}) %collective-permute-start.14) | collective-permute-done | bytes 196640 | tf_op jit(solution)/shard_map/ppermute | solution.py:416
  39.7 1.2 %collective-permute-start.18 = (bf16[4,2,4,32,128]{4,3,2,1,0:T(8,128)(2,1)S(1)}, bf16[4,2,4,32,128]{4,3,2,1,0:T(8,128)(2,1)S(1)}, u32[]{:S(2)}, u32[]{:S(2)}) collective-permute-start(bf16[4,2,4,32,128]{4,3,2,1,0:T(8,128)(2,1)S(1)} %pad_maximum_fusion.2.rest_0_.rest_2_), channel_id=1, source_target_pairs={{0,4},{4,0},{8,12},{12,8},{16,20},{20,16},{24,28},{28,24},{1,5},{5... | collective-permute-start | bytes 786440 | tf_op jit(solution)/shard_map/ppermute | solution.py:416
  41.1 0.3 collective-permute-start.17
  41.3 0.8 %collective-permute-start.16 = (bf16[2,2,4,32,128]{4,3,2,1,0:T(8,128)(2,1)S(1)}, bf16[2,2,4,32,128]{4,3,2,1,0:T(8,128)(2,1)S(1)}, u32[]{:S(2)}, u32[]{:S(2)}) collective-permute-start(bf16[2,2,4,32,128]{4,3,2,1,0:T(8,128)(2,1)S(1)} %slice.20), channel_id=1, source_target_pairs={{0,8},{4,12},{8,0},{12,4},{16,24},{20,28},{24,16},{28,20},{1,9},{5... | collective-permute-start | bytes 393224 | tf_op jit(solution)/shard_map/ppermute | solution.py:416
  42.1 2.3 %second.1 = (f32[4,4,32,192]{3,2,1,0:T(8,128)S(1)}, f32[3,576,256]{2,1,0:T(8,128)S(1)}) custom-call(s32[3]{0:T(128)S(1)} %pad_add_fusion.place, bf16[9,256,192]{2,1,0:T(8,128)(2,1)S(1)} %get-tuple-element.60.weight, bf16[4,576,1280]{2,1,0:T(8,128)(2,1)S(1)} %get-tuple-element.61.turned, f32[3,576,256]{2,1,0:T(8,128)S(1)} %get-tuple-element.66.old, ...), custom_call_target="tpu_custom_call" | custom-call | bytes 1024 | tf_op jit(solution)/shard_map/second/pallas_call | solution.py:435
  44.5 1.8 %third.1.old = f32[3,576,256]{2,1,0:T(8,128)S(1)} custom-call(s32[3]{0:T(128)S(1)} %pad_add_fusion.place, bf16[4,576,1280]{2,1,0:T(8,128)(2,1)S(1)} %get-tuple-element.61.turned, f32[3,576,256]{2,1,0:T(8,128)S(1)} %get-tuple-element.67.old, bf16[4,2,4,32,128]{4,3,2,1,0:T(8,128)(2,1)S(1)} %collective-permute-done.18.rest_0_.rest_3_, ...), custom_call_target="tpu_custom_call" | custom-call | bytes 1024 | tf_op jit(solution)/shard_map/third/pallas_call | solution.py:435
  46.3 1.1 %collective-permute-start.20 = (bf16[4,2,4,32,128]{4,3,2,1,0:T(8,128)(2,1)S(1)}, bf16[4,2,4,32,128]{4,3,2,1,0:T(8,128)(2,1)S(1)}, u32[]{:S(2)}, u32[]{:S(2)}) collective-permute-start(bf16[4,2,4,32,128]{4,3,2,1,0:T(8,128)(2,1)S(1)} %constant_dynamic-update-slice_fusion.2.rest_6_), channel_id=1, source_target_pairs={{0,4},{4,0},{8,12},{12,8},{16,20},{20,16},{24,28},{28,24},{1,5},{5... | collective-permute-start | bytes 786440 | tf_op jit(solution)/shard_map/ppermute | solution.py:416
  47.4 1.6 %rim.1 = (f32[4,4,32,192]{3,2,1,0:T(8,128)S(1)}, f32[1,128]{1,0:T(1,128)S(1)}, f32[3,576,256]{2,1,0:T(8,128)S(1)}) custom-call(s32[3]{0:T(128)S(1)} %pad_add_fusion.place, bf16[9,256,192]{2,1,0:T(8,128)(2,1)S(1)} %get-tuple-element.60.weight, bf16[4,576,1280]{2,1,0:T(8,128)(2,1)S(1)} %get-tuple-element.61.turned, f32[3,576,256]{2,1,0:T(8,128)S(1)} %third.1.old, ...), custom_call_target="tpu_custom_call" | custom-call | bytes 1024 | tf_op jit(solution)/shard_map/rim/pallas_call | solution.py:435
  49.0 2.4 %last.1 = (bf16[512,64]{1,0:T(8,128)(2,1)}, f32[3,576,256]{2,1,0:T(8,128)}, f32[1,64]{1,0:T(1,128)}) custom-call(s32[3]{0:T(128)S(1)} %pad_add_fusion.place, bf16[9,256,192]{2,1,0:T(8,128)(2,1)S(1)} %get-tuple-element.60.weight, bf16[4,576,1280]{2,1,0:T(8,128)(2,1)S(1)} %get-tuple-element.61.turned, f32[3,576,256]{2,1,0:T(8,128)S(1)} %get-tuple-element.72.old, ...), custom_call_target="tpu_custom_call" | custom-call | tf_op jit(solution)/shard_map/last/pallas_call | solution.py:549
  (34 shorter events, 0.6 us)
Async XLA Ops:
  2.3 8.3 %collective-permute-start.2 = (bf16[2,4,32,128]{3,2,1,0:T(8,128)(2,1)S(1)}, bf16[2,4,32,128]{3,2,1,0:T(8,128)(2,1)S(1)}, u32[]{:S(2)}, u32[]{:S(2)}) collective-permute-start(bf16[2,4,32,128]{3,2,1,0:T(8,128)(2,1)S(1)} %get-tuple-element.44.packed), channel_id=1, source_target_pairs={{0,16},{4,20},{8,24},{12,28},{16,0},{20,4},{24,8},{28,12},{1,17},{... | collective-permute-start | bytes 196616 | tf_op jit(solution)/shard_map/ppermute | solution.py:416
  4.4 6.2 %collective-permute-start = (bf16[4,32,64]{2,1,0:T(8,128)(2,1)S(1)}, bf16[4,32,64]{2,1,0:T(8,128)(2,1)S(1)}, u32[]{:S(2)}, u32[]{:S(2)}) collective-permute-start(bf16[4,32,64]{2,1,0:T(8,128)(2,1)S(1)} %get-tuple-element.45), channel_id=1, source_target_pairs={{0,4},{4,0},{8,12},{12,8},{16,20},{20,16},{24,28},{28,24},{1,5},{5... | collective-permute-start | bytes 49160 | tf_op jit(solution)/shard_map/ppermute | solution.py:416
  5.3 5.2 %collective-permute-start.1 = (bf16[4,32,64]{2,1,0:T(8,128)(2,1)S(1)}, bf16[4,32,64]{2,1,0:T(8,128)(2,1)S(1)}, u32[]{:S(2)}, u32[]{:S(2)}) collective-permute-start(bf16[4,32,64]{2,1,0:T(8,128)(2,1)S(1)} %get-tuple-element.46), channel_id=1, source_target_pairs={{0,12},{4,8},{8,4},{12,0},{16,28},{20,24},{24,20},{28,16},{1,13},{... | collective-permute-start | bytes 49160 | tf_op jit(solution)/shard_map/ppermute | solution.py:416
  6.4 4.1 %collective-permute-start.4 = (bf16[32,64]{1,0:T(8,128)(2,1)S(1)}, bf16[32,64]{1,0:T(8,128)(2,1)S(1)}, u32[]{:S(2)}, u32[]{:S(2)}) collective-permute-start(bf16[32,64]{1,0:T(8,128)(2,1)S(1)} %get-tuple-element.47), channel_id=1, source_target_pairs={{0,28},{4,24},{8,20},{12,16},{16,12},{20,8},{24,4},{28,0},{1,29},{... | collective-permute-start | bytes 12296 | tf_op jit(solution)/shard_map/ppermute | solution.py:416
  6.6 3.9 %collective-permute-start.3 = (bf16[32,64]{1,0:T(8,128)(2,1)S(1)}, bf16[32,64]{1,0:T(8,128)(2,1)S(1)}, u32[]{:S(2)}, u32[]{:S(2)}) collective-permute-start(bf16[32,64]{1,0:T(8,128)(2,1)S(1)} %get-tuple-element.41.after), channel_id=1, source_target_pairs={{0,20},{4,16},{8,28},{12,24},{16,4},{20,0},{24,12},{28,8},{1,21},{... | collective-permute-start | bytes 12296 | tf_op jit(solution)/shard_map/ppermute | solution.py:416
  12.2 5.1 %collective-permute-start.5 = (bf16[256,128]{1,0:T(8,128)(2,1)S(1)}, bf16[256,128]{1,0:T(8,128)(2,1)S(1)}, u32[]{:S(2)}, u32[]{:S(2)}) collective-permute-start(bf16[256,128]{1,0:T(8,128)(2,1)S(1)} %get-tuple-element.49), channel_id=1, source_target_pairs={{0,3},{1,2},{2,1},{3,0},{4,7},{5,6},{6,5},{7,4},{8,11},{9,10},{10,... | collective-permute-start | bytes 196616 | tf_op jit(solution)/shard_map/ppermute | solution.py:416
  15.6 5.7 %collective-permute-start.6 = (bf16[256,128]{1,0:T(8,128)(2,1)S(1)}, bf16[256,128]{1,0:T(8,128)(2,1)S(1)}, u32[]{:S(2)}, u32[]{:S(2)}) collective-permute-start(bf16[256,128]{1,0:T(8,128)(2,1)S(1)} %get-tuple-element.50), channel_id=1, source_target_pairs={{0,2},{1,3},{2,0},{3,1},{4,6},{5,7},{6,4},{7,5},{8,10},{9,11},{10,... | collective-permute-start | bytes 196616 | tf_op jit(solution)/shard_map/ppermute | solution.py:416
  15.6 5.7 %collective-permute-start.7 = (bf16[256,128]{1,0:T(8,128)(2,1)S(1)}, bf16[256,128]{1,0:T(8,128)(2,1)S(1)}, u32[]{:S(2)}, u32[]{:S(2)}) collective-permute-start(bf16[256,128]{1,0:T(8,128)(2,1)S(1)} %get-tuple-element.51), channel_id=1, source_target_pairs={{0,1},{1,0},{2,3},{3,2},{4,5},{5,4},{6,7},{7,6},{8,9},{9,8},{10,11... | collective-permute-start | bytes 196616 | tf_op jit(solution)/shard_map/ppermute | solution.py:416
  21.5 9.6 %collective-permute-start.8 = (bf16[3,2,4,32,128]{4,3,2,1,0:T(8,128)(2,1)S(1)}, bf16[3,2,4,32,128]{4,3,2,1,0:T(8,128)(2,1)S(1)}, u32[]{:S(2)}, u32[]{:S(2)}) collective-permute-start(bf16[3,2,4,32,128]{4,3,2,1,0:T(8,128)(2,1)S(1)} %pad_maximum_fusion.3), channel_id=1, source_target_pairs={{0,8},{4,12},{8,0},{12,4},{16,24},{20,28},{24,16},{28,20},{1,9},{5... | collective-permute-start | bytes 589832 | tf_op jit(solution)/shard_map/ppermute | solution.py:416
  22.2 4.9 %collective-permute-start.12 = (bf16[256,128]{1,0:T(8,128)(2,1)S(1)}, bf16[256,128]{1,0:T(8,128)(2,1)S(1)}, u32[]{:S(2)}, u32[]{:S(2)}) collective-permute-start(bf16[256,128]{1,0:T(8,128)(2,1)S(1)} %get-tuple-element.56), channel_id=1, source_target_pairs={{0,3},{1,2},{2,1},{3,0},{4,7},{5,6},{6,5},{7,4},{8,11},{9,10},{10,... | collective-permute-start | bytes 196616 | tf_op jit(solution)/shard_map/ppermute | solution.py:416
  24.5 6.5 %collective-permute-start.11 = (bf16[256,128]{1,0:T(8,128)(2,1)S(1)}, bf16[256,128]{1,0:T(8,128)(2,1)S(1)}, u32[]{:S(2)}, u32[]{:S(2)}) collective-permute-start(bf16[256,128]{1,0:T(8,128)(2,1)S(1)} %get-tuple-element.56), channel_id=1, source_target_pairs={{0,2},{1,3},{2,0},{3,1},{4,6},{5,7},{6,4},{7,5},{8,10},{9,11},{10,... | collective-permute-start | bytes 196616 | tf_op jit(solution)/shard_map/ppermute | solution.py:416
  24.5 6.5 %collective-permute-start.10 = (bf16[256,128]{1,0:T(8,128)(2,1)S(1)}, bf16[256,128]{1,0:T(8,128)(2,1)S(1)}, u32[]{:S(2)}, u32[]{:S(2)}) collective-permute-start(bf16[256,128]{1,0:T(8,128)(2,1)S(1)} %get-tuple-element.56), channel_id=1, source_target_pairs={{0,1},{1,0},{2,3},{3,2},{4,5},{5,4},{6,7},{7,6},{8,9},{9,8},{10,11... | collective-permute-start | bytes 196616 | tf_op jit(solution)/shard_map/ppermute | solution.py:416
  25.8 5.3 %collective-permute-start.9 = (bf16[1,2,4,32,128]{4,3,2,1,0:T(8,128)(2,1)S(1)}, bf16[1,2,4,32,128]{4,3,2,1,0:T(8,128)(2,1)S(1)}, u32[]{:S(2)}, u32[]{:S(2)}) collective-permute-start(bf16[1,2,4,32,128]{4,3,2,1,0:T(8,128)(2,1)S(1)} %bitcast.15), channel_id=1, source_target_pairs={{0,16},{4,20},{8,24},{12,28},{16,0},{20,4},{24,8},{28,12},{1,17},{... | collective-permute-start | bytes 196616 | tf_op jit(solution)/shard_map/ppermute | solution.py:416
  31.2 2.6 %collective-permute-start.13 = (bf16[8,2,4,32,128]{4,3,2,1,0:T(8,128)(2,1)S(1)}, bf16[8,2,4,32,128]{4,3,2,1,0:T(8,128)(2,1)S(1)}, u32[]{:S(2)}, u32[]{:S(2)}) collective-permute-start(bf16[8,2,4,32,128]{4,3,2,1,0:T(8,128)(2,1)S(1)} %pad_maximum_fusion), channel_id=1, source_target_pairs={{0,4},{4,0},{8,12},{12,8},{16,20},{20,16},{24,28},{28,24},{1,5},{5... | collective-permute-start | bytes 1572872 | tf_op jit(solution)/shard_map/ppermute | solution.py:416
  32.2 6.6 %collective-permute-start.15 = (bf16[3,2,4,32,128]{4,3,2,1,0:T(8,128)(2,1)S(1)}, bf16[3,2,4,32,128]{4,3,2,1,0:T(8,128)(2,1)S(1)}, u32[]{:S(2)}, u32[]{:S(2)}) collective-permute-start(bf16[3,2,4,32,128]{4,3,2,1,0:T(8,128)(2,1)S(1)} %pad_maximum_fusion.4), channel_id=1, source_target_pairs={{0,16},{4,20},{8,24},{12,28},{16,0},{20,4},{24,8},{28,12},{1,17},{... | collective-permute-start | bytes 589832 | tf_op jit(solution)/shard_map/ppermute | solution.py:416
  33.5 6.1 %collective-permute-start.14 = (bf16[3,2,4,32,128]{4,3,2,1,0:T(8,128)(2,1)S(1)}, bf16[3,2,4,32,128]{4,3,2,1,0:T(8,128)(2,1)S(1)}, u32[]{:S(2)}, u32[]{:S(2)}) collective-permute-start(bf16[3,2,4,32,128]{4,3,2,1,0:T(8,128)(2,1)S(1)} %pad_maximum_fusion.4), channel_id=1, source_target_pairs={{0,8},{4,12},{8,0},{12,4},{16,24},{20,28},{24,16},{28,20},{1,9},{5... | collective-permute-start | bytes 589832 | tf_op jit(solution)/shard_map/ppermute | solution.py:416
  39.7 4.8 %collective-permute-start.18 = (bf16[4,2,4,32,128]{4,3,2,1,0:T(8,128)(2,1)S(1)}, bf16[4,2,4,32,128]{4,3,2,1,0:T(8,128)(2,1)S(1)}, u32[]{:S(2)}, u32[]{:S(2)}) collective-permute-start(bf16[4,2,4,32,128]{4,3,2,1,0:T(8,128)(2,1)S(1)} %pad_maximum_fusion.2.rest_0_.rest_2_), channel_id=1, source_target_pairs={{0,4},{4,0},{8,12},{12,8},{16,20},{20,16},{24,28},{28,24},{1,5},{5... | collective-permute-start | bytes 786440 | tf_op jit(solution)/shard_map/ppermute | solution.py:416
  41.0 3.5 %collective-permute-start.19 = (bf16[4,2,4,32,128]{4,3,2,1,0:T(8,128)(2,1)S(1)}, bf16[4,2,4,32,128]{4,3,2,1,0:T(8,128)(2,1)S(1)}, u32[]{:S(2)}, u32[]{:S(2)}) collective-permute-start(bf16[4,2,4,32,128]{4,3,2,1,0:T(8,128)(2,1)S(1)} %constant_dynamic-update-slice_fusion.rest_1_.rest_4_), channel_id=1, source_target_pairs={{0,4},{4,0},{8,12},{12,8},{16,20},{20,16},{24,28},{28,24},{1,5},{5... | collective-permute-start | bytes 786440 | tf_op jit(solution)/shard_map/ppermute | solution.py:416
  41.1 5.2 %collective-permute-start.17 = (bf16[2,2,4,32,128]{4,3,2,1,0:T(8,128)(2,1)S(1)}, bf16[2,2,4,32,128]{4,3,2,1,0:T(8,128)(2,1)S(1)}, u32[]{:S(2)}, u32[]{:S(2)}) collective-permute-start(bf16[2,2,4,32,128]{4,3,2,1,0:T(8,128)(2,1)S(1)} %slice.17), channel_id=1, source_target_pairs={{0,16},{4,20},{8,24},{12,28},{16,0},{20,4},{24,8},{28,12},{1,17},{... | collective-permute-start | bytes 393224 | tf_op jit(solution)/shard_map/ppermute | solution.py:416
  41.3 4.9 %collective-permute-start.16 = (bf16[2,2,4,32,128]{4,3,2,1,0:T(8,128)(2,1)S(1)}, bf16[2,2,4,32,128]{4,3,2,1,0:T(8,128)(2,1)S(1)}, u32[]{:S(2)}, u32[]{:S(2)}) collective-permute-start(bf16[2,2,4,32,128]{4,3,2,1,0:T(8,128)(2,1)S(1)} %slice.20), channel_id=1, source_target_pairs={{0,8},{4,12},{8,0},{12,4},{16,24},{20,28},{24,16},{28,20},{1,9},{5... | collective-permute-start | bytes 393224 | tf_op jit(solution)/shard_map/ppermute | solution.py:416
  46.3 2.7 %collective-permute-start.20 = (bf16[4,2,4,32,128]{4,3,2,1,0:T(8,128)(2,1)S(1)}, bf16[4,2,4,32,128]{4,3,2,1,0:T(8,128)(2,1)S(1)}, u32[]{:S(2)}, u32[]{:S(2)}) collective-permute-start(bf16[4,2,4,32,128]{4,3,2,1,0:T(8,128)(2,1)S(1)} %constant_dynamic-update-slice_fusion.2.rest_6_), channel_id=1, source_target_pairs={{0,4},{4,0},{8,12},{12,8},{16,20},{20,16},{24,28},{28,24},{1,5},{5... | collective-permute-start | bytes 786440 | tf_op jit(solution)/shard_map/ppermute | solution.py:416
where the time goes:
time: 51.6 us; the launch traced here: 51.5 us
  starting transfers between devices  21.3 us (41%)
  Pallas kernels  17.8 us (34%)
  waiting for transfers between devices  11.2 us (22%)
  between operations  0.86 us (2%)
    ppermute x21, starting transfers between devices, exchange(): lax.ppermute(x, axes, [(i, i ^ mask) for i in range(lax.axis_size(axes))])  21.3 us
    ppermute x21, waiting for transfers between devices, exchange(): lax.ppermute(x, axes, [(i, i ^ mask) for i in range(lax.axis_size(axes))])  11.2 us
    pallas_call x5, Pallas kernels, call(): pl.pallas_call(kernel, out_shape=[jax.ShapeDtypeStruct(shape, kind) for s...  7.41 us
    pallas_call x1, Pallas kernels, body_gathered(): pl.pallas_call(functools.partial(first_kernel, parts_x, parts_y), out_sha...  5.03 us
    pallas_call x1, Pallas kernels, body_gathered(): pl.pallas_call(functools.partial(last_kernel, parts_y, x + y + 1, factor)...  2.42 us
    pallas_call x1, Pallas kernels, body_gathered(): pl.pallas_call(prepare_kernel, out_shape=[jax.ShapeDtypeStruct(inputs.sha...  1.54 us
    pallas_call x1, Pallas kernels, body_gathered(): pl.pallas_call(stage_kernel, out_shape=[jax.ShapeDtypeStruct(x.shape, x.d...  1.38 us
  transfers between devices with their start and end apart: 21, of which 6 were waited for; matrix products, arithmetic and copies ran while one was open for 0% of the time, Pallas kernels for 23%

commit v1 on v0

--- a/solution.py
+++ b/solution.py
@@ -99,10 +99,17 @@
     return even_at, odd_at, even_row, odd_row, x_at, x_row
 
 
-def prepare_kernel(place, source, inputs, packed, even, odd, even_corner, odd_corner, arrived):
-    copy = pltpu.make_async_copy(source, inputs, arrived)
-    copy.start()
-    copy.wait()
+def prepare_kernel(
+    place, source, weight_source, inputs, weight, packed, even, odd, even_corner, odd_corner, arrived
+):
+    copies = [pltpu.make_async_copy(source, inputs, arrived.at[0])]
+    for n in range(weight.shape[0]):
+        copies.append(
+            pltpu.make_async_copy(weight_source.at[n], weight.at[n], arrived.at[n + 1])
+        )
+    for copy in copies:
+        copy.start()
+    copies[0].wait()
     span_x, span_y, _, _ = inputs.shape
     half = span_x // 2
     _, _, even_row, odd_row, _, x_row = rim_sides(place, span_x, span_y)
@@ -111,21 +118,19 @@
     even_corner[...] = inputs[x_row, even_row]
     odd_corner[...] = inputs[x_row, odd_row]
     packed[...] = jnp.concatenate([inputs[:half], inputs[half:]], axis=3)
-
-
-def stage_kernel(after, *rest):
-    count = (len(rest) - 1) // 2
-    sources, targets, arrived = rest[:count], rest[count : 2 * count], rest[-1]
-    copies = []
-    for source, target in zip(sources, targets):
-        parts = source.shape[0] if len(source.shape) == 3 else 1
-        for n in range(parts):
-            here = pl.ds(n, 1) if parts > 1 else slice(None)
-            copies.append(
-                pltpu.make_async_copy(source.at[here], target.at[here], arrived.at[len(copies)])
-            )
+    for copy in copies[1:]:
+        copy.wait()
+
+
+def stage_kernel(after, weight, cotangent_source, bias_source, cotangent, bias, weight_turned, arrived):
+    copies = [
+        pltpu.make_async_copy(cotangent_source, cotangent, arrived.at[0]),
+        pltpu.make_async_copy(bias_source, bias, arrived.at[1]),
+    ]
     for copy in copies:
         copy.start()
+    for tap in range(weight.shape[0]):
+        weight_turned[tap] = weight[tap].T
     for copy in copies:
         copy.wait()
 
@@ -219,8 +224,8 @@
         store(a, total)
 
 
-def first_kernel(parts_x, parts_y, place, weight, active, pair, beside_y, sibling, column, *rest):
-    activation, turned, sums, weight_turned, volume, unpacked, sent = rest
+def first_kernel(parts_x, parts_y, place, active, pair, beside_y, sibling, column, *rest):
+    activation, turned, sums, volume, unpacked, sent = rest
     half, lanes = active.shape[0], active.shape[1] // 2
     unpacked[:half] = active[:, :lanes]
     unpacked[half:] = active[:, lanes:]
@@ -256,8 +261,6 @@
     def store(a, total):
         sums[a] = total
 
-    for tap in range(weight.shape[0]):
-        weight_turned[tap] = weight[tap].T
     members = (0, 1)
     add_terms(place, parts_y, members, (column, sibling.at[:shards]), turned, None, store)
     copy.wait()
@@ -376,34 +379,39 @@
         copies.append(pltpu.make_async_copy(source, target, sent.at[len(copies)]))
         copies[-1].start()
 
+    def finish_cells():
+        _, _, _, odd_row, _, x_row = rim_sides(place, span_x, span_y)
+        has_odd = (place[1] != 0) & (place[1] != parts_y - 1)
+        tap_x, tap_y = rim_taps(place, odd_row)
+        grid[...] = partial[...]
+
+        @pl.when(has_odd)
+        def _():
+            corner = facing(place, rows_of(place, pieces, facing_row(odd_row, span_y)))
+            term = jnp.dot(corner, weight[tap_x * 3 + tap_y], preferred_element_type=F32)
+            grid[x_row, odd_row] += term
+
+        summed = grid[...].reshape(span_x * span_y, span_z, 3 * lanes)
+        result = (
+            shifted(summed[..., :lanes], -1)
+            + summed[..., lanes : 2 * lanes]
+            + shifted(summed[..., 2 * lanes :], 1)
+        )
+        cells[...] = result.reshape(-1, lanes).astype(BF16)
+        send(cells, input_grad)
+        total = column[...] + channel_sum(pieces)
+        bias[...] = (total[:, :lanes] + total[:, lanes:]) * factor
+        send(bias, bias_grad)
+
     def store(a, total):
         sums[a] = total * factor
-        send(sums.at[a], kernel_grad.at[a])
+        for b in range(3):
+            here = pl.ds(b * 3 * lanes, 3 * lanes)
+            send(sums.at[a, here], kernel_grad.at[a, here])
+        if a == 0:
+            finish_cells()
 
     add_terms(place, parts_y, (member,), (pieces,), turned, old, store)
-
-    _, _, _, odd_row, _, x_row = rim_sides(place, span_x, span_y)
-    has_odd = (place[1] != 0) & (place[1] != parts_y - 1)
-    tap_x, tap_y = rim_taps(place, odd_row)
-    grid[...] = partial[...]
-
-    @pl.when(has_odd)
-    def _():
-        corner = facing(place, rows_of(place, pieces, facing_row(odd_row, span_y)))
-        term = jnp.dot(corner, weight[tap_x * 3 + tap_y], preferred_element_type=F32)
-        grid[x_row, odd_row] += term
-
-    summed = grid[...].reshape(span_x * span_y, span_z, 3 * lanes)
-    result = (
-        shifted(summed[..., :lanes], -1)
-        + summed[..., lanes : 2 * lanes]
-        + shifted(summed[..., 2 * lanes :], 1)
-    )
-    cells[...] = result.reshape(-1, lanes).astype(BF16)
-    send(cells, input_grad)
-    total = column[...] + channel_sum(pieces)
-    bias[...] = (total[:, :lanes] + total[:, lanes:]) * factor
-    send(bias, bias_grad)
     for copy in copies:
         copy.wait()
 
@@ -444,27 +452,17 @@
         )(*args)
 
     row = (span_x, span_z, local_ch)
-    held, packed, even, odd, even_corner, odd_corner = pl.pallas_call(
+    sources = [pltpu.with_memory_space_constraint(array, pltpu.HBM) for array in (inputs, taps)]
+    shapes = [inputs.shape, taps.shape, packing, row, row, row[1:], row[1:]]
+    held, taps, packed, even, odd, even_corner, odd_corner = pl.pallas_call(
         prepare_kernel,
-        out_shape=[jax.ShapeDtypeStruct(inputs.shape, BF16), jax.ShapeDtypeStruct(packing, BF16)]
-        + [jax.ShapeDtypeStruct(row, BF16)] * 2
-        + [jax.ShapeDtypeStruct(row[1:], BF16)] * 2,
-        in_specs=[SMEM, HBM],
-        out_specs=[VMEM] * 6,
-        scratch_shapes=[pltpu.SemaphoreType.DMA],
+        out_shape=[jax.ShapeDtypeStruct(shape, BF16) for shape in shapes],
+        in_specs=[SMEM, HBM, HBM],
+        out_specs=[VMEM] * len(shapes),
+        scratch_shapes=[pltpu.SemaphoreType.DMA((1 + taps.shape[0],))],
         compiler_params=PARAMS,
         name="prepare",
-    )(place, pltpu.with_memory_space_constraint(inputs, pltpu.HBM))
-    sources = (taps, cotangent.reshape(local, local_ch), bias.reshape(1, local_ch))
-    taps, cotangent, bias = pl.pallas_call(
-        stage_kernel,
-        out_shape=[jax.ShapeDtypeStruct(x.shape, x.dtype) for x in sources],
-        in_specs=[VMEM] + [HBM] * len(sources),
-        out_specs=[VMEM] * len(sources),
-        scratch_shapes=[pltpu.SemaphoreType.DMA((len(sources) + 8,))],
-        compiler_params=PARAMS,
-        name="stage",
-    )(even_corner, *[pltpu.with_memory_space_constraint(x, pltpu.HBM) for x in sources])
+    )(place, *sources)
     beside = exchange(packed, axes, parts_y)
     even = exchange(even, axes, 1)
     odd = exchange(odd, axes, 3)
@@ -477,6 +475,21 @@
         [place, taps, held, packed, even, odd, beside, even_corner, odd_corner],
         [((span_x + 2, span_y + 2, span_z, 3 * local_ch), BF16), ((shards,) + flat, F32)],
     )
+    sources = (cotangent.reshape(local, local_ch), bias.reshape(1, local_ch))
+    turned_weight_shape = (9, channels, 3 * local_ch)
+    cotangent, bias, taps_turned = pl.pallas_call(
+        stage_kernel,
+        out_shape=[
+            *[jax.ShapeDtypeStruct(array.shape, BF16) for array in sources],
+            jax.ShapeDtypeStruct(turned_weight_shape, BF16),
+        ],
+        in_specs=[VMEM, VMEM, HBM, HBM],
+        out_specs=[VMEM] * 3,
+        scratch_shapes=[pltpu.SemaphoreType.DMA((2,))],
+        compiler_params=PARAMS,
+        cost_estimate=pl.CostEstimate(flops=0, bytes_accessed=1024, transcendentals=0),
+        name="stage",
+    )(own, taps, *[pltpu.with_memory_space_constraint(array, pltpu.HBM) for array in sources])
     others = [exchange(others[k - 1], "ch", k) for k in range(shards - 1, 0, -1)]
     active, slope = call(
         slope_kernel,
@@ -497,13 +510,12 @@
     turned_shape = (parts_y, 9 * local_ch, (parts_x * span_x + 2) * span_y * span_z)
     sums_shape = (3, 9 * local_ch, channels)
     first_outs = [((local, local_ch), BF16), (turned_shape, BF16), (sums_shape, F32)]
-    first_outs += [((9, channels, 3 * local_ch), BF16)]
-    args = [place, taps, active, pair, beside_y, sibling, column]
-    activation, turned, sums, taps = pl.pallas_call(
+    args = [place, active, pair, beside_y, sibling, column]
+    activation, turned, sums = pl.pallas_call(
         functools.partial(first_kernel, parts_x, parts_y),
         out_shape=[jax.ShapeDtypeStruct(shape, kind) for shape, kind in first_outs],
         in_specs=[SMEM] + [VMEM] * (len(args) - 1),
-        out_specs=[HBM] + [VMEM] * 3,
+        out_specs=[HBM] + [VMEM] * 2,
         scratch_shapes=[
             pltpu.VMEM((parts_x * span_x + 2, parts_y * span_y + 2, span_z, 3 * local_ch), BF16),
             pltpu.VMEM((local, local_ch), BF16),
@@ -525,7 +537,7 @@
         functools.partial(second_kernel, parts_y, (y, x)),
         "second",
         [(grid_shape, F32), (sums_shape, F32)],
-        [place, taps, turned, sums, column, sibling, slopes[y], slopes[x]],
+        [place, taps_turned, turned, sums, column, sibling, slopes[y], slopes[x]],
         [((span_x + 2, span_y + 2, span_z, channels), BF16)],
     )
     slopes[y + 1], slopes[x + 1] = across
@@ -542,10 +554,10 @@
         functools.partial(rim_kernel, parts_y, (x + y,)),
         "rim",
         [(grid_shape, F32), ((1, 2 * local_ch), F32), (sums_shape, F32)],
-        [place, taps, turned, sums, partial] + [slopes[m] for m in range(count - 1)],
+        [place, taps_turned, turned, sums, partial] + [slopes[m] for m in range(count - 1)],
         [((span_y + 2, span_z, channels), BF16), ((span_x + 2, span_z, channels), BF16)],
     )
-    args = [place, taps, turned, sums, partial, column, final]
+    args = [place, taps_turned, turned, sums, partial, column, final]
     input_grad, kernel_grad, bias_grad = pl.pallas_call(
         functools.partial(last_kernel, parts_y, x + y + 1, factor),
         out_shape=[
@@ -560,7 +572,7 @@
             pltpu.VMEM(sums_shape, F32),
             pltpu.VMEM((local, local_ch), BF16),
             pltpu.VMEM((1, local_ch), F32),
-            pltpu.SemaphoreType.DMA((5,)),
+            pltpu.SemaphoreType.DMA((11,)),
         ],
         compiler_params=PARAMS,
         name="last",

time: 51.6 us -> 52.8 us (1.023)
  starting transfers between devices: 21.3 us -> 22.1 us
    ppermute x21, starting transfers between devices: 21.3 us -> 22.1 us  [exchange(): lax.ppermute(x, axes, [(i, i ^ mask) for i in range(lax.axis_size(axes))])]
  transfers between devices with their start and end apart: 21 -> 21, of which waited for: 6 -> 6; matrix products, arithmetic and copies ran while one was open for 0% -> 0% of each run, Pallas kernels for 23% -> 22%
where the time goes in v1:
time: 52.8 us; the launch traced here: 52.6 us
  starting transfers between devices  22.1 us (42%)
  Pallas kernels  18 us (34%)
  waiting for transfers between devices  11.3 us (21%)
  between operations  0.87 us (2%)
    ppermute x21, starting transfers between devices, exchange(): lax.ppermute(x, axes, [(i, i ^ mask) for i in range(lax.axis_size(axes))])  22.1 us
    ppermute x21, waiting for transfers between devices, exchange(): lax.ppermute(x, axes, [(i, i ^ mask) for i in range(lax.axis_size(axes))])  11.3 us
    pallas_call x5, Pallas kernels, call(): pl.pallas_call(kernel, out_shape=[jax.ShapeDtypeStruct(shape, kind) for s...  7.41 us
    pallas_call x1, Pallas kernels, body_gathered(): pl.pallas_call(functools.partial(first_kernel, parts_x, parts_y), out_sha...  4.98 us
    pallas_call x1, Pallas kernels, body_gathered(): pl.pallas_call(functools.partial(last_kernel, parts_y, x + y + 1, factor)...  2.81 us
    pallas_call x1, Pallas kernels, body_gathered(): pl.pallas_call(prepare_kernel, out_shape=[jax.ShapeDtypeStruct(shape, BF1...  1.9 us
  transfers between devices with their start and end apart: 21, of which 6 were waited for; matrix products, arithmetic and copies ran while one was open for 0% of the time, Pallas kernels for 22%

profile of v1, /device:TPU:1, one launch (start us, length us, event | category | flops | bytes accessed | tf_op | source)
XLA Modules:
  0.0 52.6 jit_solution(11211251675073668876)
XLA Ops:
  0.7 1.9 %prepare.1 = (bf16[4,4,32,64]{3,2,1,0:T(8,128)(2,1)S(1)}, bf16[9,192,256]{2,1,0:T(8,128)(2,1)S(1)}, bf16[2,4,32,128]{3,2,1,0:T(8,128)(2,1)S(1)}, bf16[4,32,64]{2...) custom-call(s32[3]{0:T(128)S(1)} %pad_add_fusion.place, ...), custom_call_target="tpu_custom_call" | custom-call | tf_op jit(solution)/shard_map/prepare/pallas_call | solution.py:457
  2.6 2.1 %collective-permute-start.2 = (bf16[2,4,32,128]{3,2,1,0:T(8,128)(2,1)S(1)}, bf16[2,4,32,128]{3,2,1,0:T(8,128)(2,1)S(1)}, u32[]{:S(2)}, u32[]{:S(2)}) collective-permute-start(bf16[2,4,32,128]{3,2,1,0:T(8,128)(2,1)S(1)} %get-tuple-element.43.packed), channel_id=1, source_target_pairs={{0,16},{4,20},{8,24},{12,28},{16,0},{20,4},{24,8},{28,12},{1,17},{... | collective-permute-start | bytes 196616 | tf_op jit(solution)/shard_map/ppermute | solution.py:424
  4.7 1.0 %collective-permute-start = (bf16[4,32,64]{2,1,0:T(8,128)(2,1)S(1)}, bf16[4,32,64]{2,1,0:T(8,128)(2,1)S(1)}, u32[]{:S(2)}, u32[]{:S(2)}) collective-permute-start(bf16[4,32,64]{2,1,0:T(8,128)(2,1)S(1)} %get-tuple-element.44), channel_id=1, source_target_pairs={{0,4},{4,0},{8,12},{12,8},{16,20},{20,16},{24,28},{28,24},{1,5},{5... | collective-permute-start | bytes 49160 | tf_op jit(solution)/shard_map/ppermute | solution.py:424
  5.7 1.1 %collective-permute-start.1 = (bf16[4,32,64]{2,1,0:T(8,128)(2,1)S(1)}, bf16[4,32,64]{2,1,0:T(8,128)(2,1)S(1)}, u32[]{:S(2)}, u32[]{:S(2)}) collective-permute-start(bf16[4,32,64]{2,1,0:T(8,128)(2,1)S(1)} %get-tuple-element.45), channel_id=1, source_target_pairs={{0,12},{4,8},{8,4},{12,0},{16,28},{20,24},{24,20},{28,16},{1,13},{... | collective-permute-start | bytes 49160 | tf_op jit(solution)/shard_map/ppermute | solution.py:424
  6.8 0.6 %collective-permute-start.3 = (bf16[32,64]{1,0:T(8,128)(2,1)S(1)}, bf16[32,64]{1,0:T(8,128)(2,1)S(1)}, u32[]{:S(2)}, u32[]{:S(2)}) collective-permute-start(bf16[32,64]{1,0:T(8,128)(2,1)S(1)} %get-tuple-element.46), channel_id=1, source_target_pairs={{0,20},{4,16},{8,28},{12,24},{16,4},{20,0},{24,12},{28,8},{1,21},{... | collective-permute-start | bytes 12296 | tf_op jit(solution)/shard_map/ppermute | solution.py:424
  7.5 1.0 %collective-permute-start.4 = (bf16[32,64]{1,0:T(8,128)(2,1)S(1)}, bf16[32,64]{1,0:T(8,128)(2,1)S(1)}, u32[]{:S(2)}, u32[]{:S(2)}) collective-permute-start(bf16[32,64]{1,0:T(8,128)(2,1)S(1)} %get-tuple-element.47), channel_id=1, source_target_pairs={{0,28},{4,24},{8,20},{12,16},{16,12},{20,8},{24,4},{28,0},{1,29},{... | collective-permute-start | bytes 12296 | tf_op jit(solution)/shard_map/ppermute | solution.py:424
  8.5 1.5 %collective-permute-done.3.even_corner = bf16[32,64]{1,0:T(8,128)(2,1)S(1)} collective-permute-done((bf16[32,64]{1,0:T(8,128)(2,1)S(1)}, bf16[32,64]{1,0:T(8,128)(2,1)S(1)}, u32[]{:S(2)}, u32[]{:S(2)}) %collective-permute-start.3) | collective-permute-done | bytes 4128 | tf_op jit(solution)/shard_map/ppermute | solution.py:424
  10.0 1.4 %collective-permute-done.4.odd_corner = bf16[32,64]{1,0:T(8,128)(2,1)S(1)} collective-permute-done((bf16[32,64]{1,0:T(8,128)(2,1)S(1)}, bf16[32,64]{1,0:T(8,128)(2,1)S(1)}, u32[]{:S(2)}, u32[]{:S(2)}) %collective-permute-start.4) | collective-permute-done | bytes 4128 | tf_op jit(solution)/shard_map/ppermute | solution.py:424
  11.4 1.6 %forward.1 = (f32[256,128]{1,0:T(8,128)S(1)}, bf16[256,128]{1,0:T(8,128)(2,1)S(1)}, bf16[256,128]{1,0:T(8,128)(2,1)S(1)}, bf16[256,128]{1,0:T(8,128)(2,1)S(1)}, bf16[2,2,4,32,128]{4,3,2,1,0:T(8,128)(2,1)S(1)}) custom-call(s32[3]{0:T(128)S(1)} %pad_add_fusion.place, bf16[9,192,256]{2,1,0:T(8,128)(2,1)S(1)} %get-tuple-element.41.weight, ...), custom_call_target="tpu_custom_call" | custom-call | bytes 1024 | tf_op jit(solution)/shard_map/forward/pallas_call | solution.py:443
  13.1 3.4 %collective-permute-start.5 = (bf16[256,128]{1,0:T(8,128)(2,1)S(1)}, bf16[256,128]{1,0:T(8,128)(2,1)S(1)}, u32[]{:S(2)}, u32[]{:S(2)}) collective-permute-start(bf16[256,128]{1,0:T(8,128)(2,1)S(1)} %get-tuple-element.49), channel_id=1, source_target_pairs={{0,3},{1,2},{2,1},{3,0},{4,7},{5,6},{6,5},{7,4},{8,11},{9,10},{10,... | collective-permute-start | bytes 196616 | tf_op jit(solution)/shard_map/ppermute | solution.py:424
  16.5 0.4 collective-permute-start.7
  16.8 0.9 %stage.1 = (bf16[512,64]{1,0:T(8,128)(2,1)S(1)}, bf16[1,64]{1,0:T(2,128)(2,1)S(1)}, bf16[9,256,192]{2,1,0:T(8,128)(2,1)S(1)}) custom-call(f32[256,128]{1,0:T(8,128)S(1)} %get-tuple-element.48.after.own, bf16[9,192,256]{2,1,0:T(8,128)(2,1)S(1)} %get-tuple-element.41.weight, bf16[512,64]{1,0:T(8,128)(2,1)} %bitcast.19, bf16[1,64]{1,0:T(2,128)(2,1)} %bitcast.23), custom_call_target="tpu_custom_call" | custom-call | bytes 1024 | tf_op jit(solution)/shard_map/stage/pallas_call | solution.py:480
  17.8 1.1 %collective-permute-done.5.rest_0_ = bf16[256,128]{1,0:T(8,128)(2,1)S(1)} collective-permute-done((bf16[256,128]{1,0:T(8,128)(2,1)S(1)}, bf16[256,128]{1,0:T(8,128)(2,1)S(1)}, u32[]{:S(2)}, u32[]{:S(2)}) %collective-permute-start.5) | collective-permute-done | bytes 65568 | tf_op jit(solution)/shard_map/ppermute | solution.py:424
  18.9 3.2 %collective-permute-done.6.rest_1_ = bf16[256,128]{1,0:T(8,128)(2,1)S(1)} collective-permute-done((bf16[256,128]{1,0:T(8,128)(2,1)S(1)}, bf16[256,128]{1,0:T(8,128)(2,1)S(1)}, u32[]{:S(2)}, u32[]{:S(2)}) %collective-permute-start.6) | collective-permute-done | bytes 65568 | tf_op jit(solution)/shard_map/ppermute | solution.py:424
  22.3 0.3 collective-permute-start.8
  22.6 2.2 %collective-permute-start.12 = (bf16[256,128]{1,0:T(8,128)(2,1)S(1)}, bf16[256,128]{1,0:T(8,128)(2,1)S(1)}, u32[]{:S(2)}, u32[]{:S(2)}) collective-permute-start(bf16[256,128]{1,0:T(8,128)(2,1)S(1)} %get-tuple-element.56), channel_id=1, source_target_pairs={{0,3},{1,2},{2,1},{3,0},{4,7},{5,6},{6,5},{7,4},{8,11},{9,10},{10,... | collective-permute-start | bytes 196616 | tf_op jit(solution)/shard_map/ppermute | solution.py:424
  24.8 1.3 %collective-permute-start.10 = (bf16[256,128]{1,0:T(8,128)(2,1)S(1)}, bf16[256,128]{1,0:T(8,128)(2,1)S(1)}, u32[]{:S(2)}, u32[]{:S(2)}) collective-permute-start(bf16[256,128]{1,0:T(8,128)(2,1)S(1)} %get-tuple-element.56), channel_id=1, source_target_pairs={{0,1},{1,0},{2,3},{3,2},{4,5},{5,4},{6,7},{7,6},{8,9},{9,8},{10,11... | collective-permute-start | bytes 196616 | tf_op jit(solution)/shard_map/ppermute | solution.py:424
  26.1 1.2 %collective-permute-start.9 = (bf16[1,2,4,32,128]{4,3,2,1,0:T(8,128)(2,1)S(1)}, bf16[1,2,4,32,128]{4,3,2,1,0:T(8,128)(2,1)S(1)}, u32[]{:S(2)}, u32[]{:S(2)}) collective-permute-start(bf16[1,2,4,32,128]{4,3,2,1,0:T(8,128)(2,1)S(1)} %bitcast.15), channel_id=1, source_target_pairs={{0,16},{4,20},{8,24},{12,28},{16,0},{20,4},{24,8},{28,12},{1,17},{... | collective-permute-start | bytes 196616 | tf_op jit(solution)/shard_map/ppermute | solution.py:424
  27.3 0.2 collective-permute-done.12
  27.5 3.9 %collective-permute-done.11 = bf16[256,128]{1,0:T(8,128)(2,1)S(1)} collective-permute-done((bf16[256,128]{1,0:T(8,128)(2,1)S(1)}, bf16[256,128]{1,0:T(8,128)(2,1)S(1)}, u32[]{:S(2)}, u32[]{:S(2)}) %collective-permute-start.11) | collective-permute-done | bytes 65568 | tf_op jit(solution)/shard_map/ppermute | solution.py:424
  31.5 1.1 %collective-permute-start.13 = (bf16[8,2,4,32,128]{4,3,2,1,0:T(8,128)(2,1)S(1)}, bf16[8,2,4,32,128]{4,3,2,1,0:T(8,128)(2,1)S(1)}, u32[]{:S(2)}, u32[]{:S(2)}) collective-permute-start(bf16[8,2,4,32,128]{4,3,2,1,0:T(8,128)(2,1)S(1)} %pad_maximum_fusion), channel_id=1, source_target_pairs={{0,4},{4,0},{8,12},{12,8},{16,20},{20,16},{24,28},{28,24},{1,5},{5... | collective-permute-start | bytes 1572872 | tf_op jit(solution)/shard_map/ppermute | solution.py:424
  32.6 1.2 %collective-permute-start.15 = (bf16[3,2,4,32,128]{4,3,2,1,0:T(8,128)(2,1)S(1)}, bf16[3,2,4,32,128]{4,3,2,1,0:T(8,128)(2,1)S(1)}, u32[]{:S(2)}, u32[]{:S(2)}) collective-permute-start(bf16[3,2,4,32,128]{4,3,2,1,0:T(8,128)(2,1)S(1)} %pad_maximum_fusion.4), channel_id=1, source_target_pairs={{0,16},{4,20},{8,24},{12,28},{16,0},{20,4},{24,8},{28,12},{1,17},{... | collective-permute-start | bytes 589832 | tf_op jit(solution)/shard_map/ppermute | solution.py:424
  33.8 1.2 %collective-permute-start.14 = (bf16[3,2,4,32,128]{4,3,2,1,0:T(8,128)(2,1)S(1)}, bf16[3,2,4,32,128]{4,3,2,1,0:T(8,128)(2,1)S(1)}, u32[]{:S(2)}, u32[]{:S(2)}) collective-permute-start(bf16[3,2,4,32,128]{4,3,2,1,0:T(8,128)(2,1)S(1)} %pad_maximum_fusion.4), channel_id=1, source_target_pairs={{0,8},{4,12},{8,0},{12,4},{16,24},{20,28},{24,16},{28,20},{1,9},{5... | collective-permute-start | bytes 589832 | tf_op jit(solution)/shard_map/ppermute | solution.py:424
  35.1 5.0 %first.1 = (bf16[512,64]{1,0:T(8,128)(2,1)}, bf16[4,576,1280]{2,1,0:T(8,128)(2,1)S(1)}, f32[3,576,256]{2,1,0:T(8,128)S(1)}) custom-call(s32[3]{0:T(128)S(1)} %pad_add_fusion.place, bf16[256,128]{1,0:T(8,128)(2,1)S(1)} %get-tuple-element.54.active, bf16[2,2,4,32,128]{4,3,2,1,0:T(8,128)(2,1)S(1)} %get-tuple-element.55.pair, ...), custom_call_target="tpu_custom_call" | custom-call | bytes 1024 | tf_op jit(solution)/shard_map/first/pallas_call | solution.py:514
  40.2 1.1 %collective-permute-start.18 = (bf16[4,2,4,32,128]{4,3,2,1,0:T(8,128)(2,1)S(1)}, bf16[4,2,4,32,128]{4,3,2,1,0:T(8,128)(2,1)S(1)}, u32[]{:S(2)}, u32[]{:S(2)}) collective-permute-start(bf16[4,2,4,32,128]{4,3,2,1,0:T(8,128)(2,1)S(1)} %pad_maximum_fusion.2.rest_0_.rest_2_), channel_id=1, source_target_pairs={{0,4},{4,0},{8,12},{12,8},{16,20},{20,16},{24,28},{28,24},{1,5},{5... | collective-permute-start | bytes 786440 | tf_op jit(solution)/shard_map/ppermute | solution.py:424
  41.4 0.3 collective-permute-start.17
  41.7 1.2 %collective-permute-start.16 = (bf16[2,2,4,32,128]{4,3,2,1,0:T(8,128)(2,1)S(1)}, bf16[2,2,4,32,128]{4,3,2,1,0:T(8,128)(2,1)S(1)}, u32[]{:S(2)}, u32[]{:S(2)}) collective-permute-start(bf16[2,2,4,32,128]{4,3,2,1,0:T(8,128)(2,1)S(1)} %slice.20), channel_id=1, source_target_pairs={{0,8},{4,12},{8,0},{12,4},{16,24},{20,28},{24,16},{28,20},{1,9},{5... | collective-permute-start | bytes 393224 | tf_op jit(solution)/shard_map/ppermute | solution.py:424
  42.9 2.3 %second.1 = (f32[4,4,32,192]{3,2,1,0:T(8,128)S(1)}, f32[3,576,256]{2,1,0:T(8,128)S(1)}) custom-call(s32[3]{0:T(128)S(1)} %pad_add_fusion.place, bf16[9,256,192]{2,1,0:T(8,128)(2,1)S(1)} %get-tuple-element.60.weight, bf16[4,576,1280]{2,1,0:T(8,128)(2,1)S(1)} %get-tuple-element.61.turned, f32[3,576,256]{2,1,0:T(8,128)S(1)} %get-tuple-element.66.old, ...), custom_call_target="tpu_custom_call" | custom-call | bytes 1024 | tf_op jit(solution)/shard_map/second/pallas_call | solution.py:443
  45.3 1.8 %third.1.old = f32[3,576,256]{2,1,0:T(8,128)S(1)} custom-call(s32[3]{0:T(128)S(1)} %pad_add_fusion.place, bf16[4,576,1280]{2,1,0:T(8,128)(2,1)S(1)} %get-tuple-element.61.turned, f32[3,576,256]{2,1,0:T(8,128)S(1)} %get-tuple-element.67.old, bf16[4,2,4,32,128]{4,3,2,1,0:T(8,128)(2,1)S(1)} %collective-permute-done.18.rest_0_.rest_3_, ...), custom_call_target="tpu_custom_call" | custom-call | bytes 1024 | tf_op jit(solution)/shard_map/third/pallas_call | solution.py:443
  47.1 1.1 %collective-permute-start.20 = (bf16[4,2,4,32,128]{4,3,2,1,0:T(8,128)(2,1)S(1)}, bf16[4,2,4,32,128]{4,3,2,1,0:T(8,128)(2,1)S(1)}, u32[]{:S(2)}, u32[]{:S(2)}) collective-permute-start(bf16[4,2,4,32,128]{4,3,2,1,0:T(8,128)(2,1)S(1)} %constant_dynamic-update-slice_fusion.2.rest_6_), channel_id=1, source_target_pairs={{0,4},{4,0},{8,12},{12,8},{16,20},{20,16},{24,28},{28,24},{1,5},{5... | collective-permute-start | bytes 786440 | tf_op jit(solution)/shard_map/ppermute | solution.py:424
  48.2 1.6 %rim.1 = (f32[4,4,32,192]{3,2,1,0:T(8,128)S(1)}, f32[1,128]{1,0:T(1,128)S(1)}, f32[3,576,256]{2,1,0:T(8,128)S(1)}) custom-call(s32[3]{0:T(128)S(1)} %pad_add_fusion.place, bf16[9,256,192]{2,1,0:T(8,128)(2,1)S(1)} %get-tuple-element.60.weight, bf16[4,576,1280]{2,1,0:T(8,128)(2,1)S(1)} %get-tuple-element.61.turned, f32[3,576,256]{2,1,0:T(8,128)S(1)} %third.1.old, ...), custom_call_target="tpu_custom_call" | custom-call | bytes 1024 | tf_op jit(solution)/shard_map/rim/pallas_call | solution.py:443
  49.8 2.8 %last.1 = (bf16[512,64]{1,0:T(8,128)(2,1)}, f32[3,576,256]{2,1,0:T(8,128)}, f32[1,64]{1,0:T(1,128)}) custom-call(s32[3]{0:T(128)S(1)} %pad_add_fusion.place, bf16[9,256,192]{2,1,0:T(8,128)(2,1)S(1)} %get-tuple-element.60.weight, bf16[4,576,1280]{2,1,0:T(8,128)(2,1)S(1)} %get-tuple-element.61.turned, f32[3,576,256]{2,1,0:T(8,128)S(1)} %get-tuple-element.72.old, ...), custom_call_target="tpu_custom_call" | custom-call | tf_op jit(solution)/shard_map/last/pallas_call | solution.py:561
  (34 shorter events, 0.6 us)
Async XLA Ops:
  2.6 8.8 %collective-permute-start.2 = (bf16[2,4,32,128]{3,2,1,0:T(8,128)(2,1)S(1)}, bf16[2,4,32,128]{3,2,1,0:T(8,128)(2,1)S(1)}, u32[]{:S(2)}, u32[]{:S(2)}) collective-permute-start(bf16[2,4,32,128]{3,2,1,0:T(8,128)(2,1)S(1)} %get-tuple-element.43.packed), channel_id=1, source_target_pairs={{0,16},{4,20},{8,24},{12,28},{16,0},{20,4},{24,8},{28,12},{1,17},{... | collective-permute-start | bytes 196616 | tf_op jit(solution)/shard_map/ppermute | solution.py:424
  4.7 6.7 %collective-permute-start = (bf16[4,32,64]{2,1,0:T(8,128)(2,1)S(1)}, bf16[4,32,64]{2,1,0:T(8,128)(2,1)S(1)}, u32[]{:S(2)}, u32[]{:S(2)}) collective-permute-start(bf16[4,32,64]{2,1,0:T(8,128)(2,1)S(1)} %get-tuple-element.44), channel_id=1, source_target_pairs={{0,4},{4,0},{8,12},{12,8},{16,20},{20,16},{24,28},{28,24},{1,5},{5... | collective-permute-start | bytes 49160 | tf_op jit(solution)/shard_map/ppermute | solution.py:424
  5.7 5.8 %collective-permute-start.1 = (bf16[4,32,64]{2,1,0:T(8,128)(2,1)S(1)}, bf16[4,32,64]{2,1,0:T(8,128)(2,1)S(1)}, u32[]{:S(2)}, u32[]{:S(2)}) collective-permute-start(bf16[4,32,64]{2,1,0:T(8,128)(2,1)S(1)} %get-tuple-element.45), channel_id=1, source_target_pairs={{0,12},{4,8},{8,4},{12,0},{16,28},{20,24},{24,20},{28,16},{1,13},{... | collective-permute-start | bytes 49160 | tf_op jit(solution)/shard_map/ppermute | solution.py:424
  6.8 3.2 %collective-permute-start.3 = (bf16[32,64]{1,0:T(8,128)(2,1)S(1)}, bf16[32,64]{1,0:T(8,128)(2,1)S(1)}, u32[]{:S(2)}, u32[]{:S(2)}) collective-permute-start(bf16[32,64]{1,0:T(8,128)(2,1)S(1)} %get-tuple-element.46), channel_id=1, source_target_pairs={{0,20},{4,16},{8,28},{12,24},{16,4},{20,0},{24,12},{28,8},{1,21},{... | collective-permute-start | bytes 12296 | tf_op jit(solution)/shard_map/ppermute | solution.py:424
  7.5 4.0 %collective-permute-start.4 = (bf16[32,64]{1,0:T(8,128)(2,1)S(1)}, bf16[32,64]{1,0:T(8,128)(2,1)S(1)}, u32[]{:S(2)}, u32[]{:S(2)}) collective-permute-start(bf16[32,64]{1,0:T(8,128)(2,1)S(1)} %get-tuple-element.47), channel_id=1, source_target_pairs={{0,28},{4,24},{8,20},{12,16},{16,12},{20,8},{24,4},{28,0},{1,29},{... | collective-permute-start | bytes 12296 | tf_op jit(solution)/shard_map/ppermute | solution.py:424
  13.1 5.8 %collective-permute-start.5 = (bf16[256,128]{1,0:T(8,128)(2,1)S(1)}, bf16[256,128]{1,0:T(8,128)(2,1)S(1)}, u32[]{:S(2)}, u32[]{:S(2)}) collective-permute-start(bf16[256,128]{1,0:T(8,128)(2,1)S(1)} %get-tuple-element.49), channel_id=1, source_target_pairs={{0,3},{1,2},{2,1},{3,0},{4,7},{5,6},{6,5},{7,4},{8,11},{9,10},{10,... | collective-permute-start | bytes 196616 | tf_op jit(solution)/shard_map/ppermute | solution.py:424
  16.5 5.6 %collective-permute-start.6 = (bf16[256,128]{1,0:T(8,128)(2,1)S(1)}, bf16[256,128]{1,0:T(8,128)(2,1)S(1)}, u32[]{:S(2)}, u32[]{:S(2)}) collective-permute-start(bf16[256,128]{1,0:T(8,128)(2,1)S(1)} %get-tuple-element.50), channel_id=1, source_target_pairs={{0,2},{1,3},{2,0},{3,1},{4,6},{5,7},{6,4},{7,5},{8,10},{9,11},{10,... | collective-permute-start | bytes 196616 | tf_op jit(solution)/shard_map/ppermute | solution.py:424
  16.5 5.6 %collective-permute-start.7 = (bf16[256,128]{1,0:T(8,128)(2,1)S(1)}, bf16[256,128]{1,0:T(8,128)(2,1)S(1)}, u32[]{:S(2)}, u32[]{:S(2)}) collective-permute-start(bf16[256,128]{1,0:T(8,128)(2,1)S(1)} %get-tuple-element.51), channel_id=1, source_target_pairs={{0,1},{1,0},{2,3},{3,2},{4,5},{5,4},{6,7},{7,6},{8,9},{9,8},{10,11... | collective-permute-start | bytes 196616 | tf_op jit(solution)/shard_map/ppermute | solution.py:424
  22.3 9.1 %collective-permute-start.8 = (bf16[3,2,4,32,128]{4,3,2,1,0:T(8,128)(2,1)S(1)}, bf16[3,2,4,32,128]{4,3,2,1,0:T(8,128)(2,1)S(1)}, u32[]{:S(2)}, u32[]{:S(2)}) collective-permute-start(bf16[3,2,4,32,128]{4,3,2,1,0:T(8,128)(2,1)S(1)} %pad_maximum_fusion.3), channel_id=1, source_target_pairs={{0,8},{4,12},{8,0},{12,4},{16,24},{20,28},{24,16},{28,20},{1,9},{5... | collective-permute-start | bytes 589832 | tf_op jit(solution)/shard_map/ppermute | solution.py:424
  22.6 4.9 %collective-permute-start.12 = (bf16[256,128]{1,0:T(8,128)(2,1)S(1)}, bf16[256,128]{1,0:T(8,128)(2,1)S(1)}, u32[]{:S(2)}, u32[]{:S(2)}) collective-permute-start(bf16[256,128]{1,0:T(8,128)(2,1)S(1)} %get-tuple-element.56), channel_id=1, source_target_pairs={{0,3},{1,2},{2,1},{3,0},{4,7},{5,6},{6,5},{7,4},{8,11},{9,10},{10,... | collective-permute-start | bytes 196616 | tf_op jit(solution)/shard_map/ppermute | solution.py:424
  24.8 6.6 %collective-permute-start.11 = (bf16[256,128]{1,0:T(8,128)(2,1)S(1)}, bf16[256,128]{1,0:T(8,128)(2,1)S(1)}, u32[]{:S(2)}, u32[]{:S(2)}) collective-permute-start(bf16[256,128]{1,0:T(8,128)(2,1)S(1)} %get-tuple-element.56), channel_id=1, source_target_pairs={{0,2},{1,3},{2,0},{3,1},{4,6},{5,7},{6,4},{7,5},{8,10},{9,11},{10,... | collective-permute-start | bytes 196616 | tf_op jit(solution)/shard_map/ppermute | solution.py:424
  24.8 6.6 %collective-permute-start.10 = (bf16[256,128]{1,0:T(8,128)(2,1)S(1)}, bf16[256,128]{1,0:T(8,128)(2,1)S(1)}, u32[]{:S(2)}, u32[]{:S(2)}) collective-permute-start(bf16[256,128]{1,0:T(8,128)(2,1)S(1)} %get-tuple-element.56), channel_id=1, source_target_pairs={{0,1},{1,0},{2,3},{3,2},{4,5},{5,4},{6,7},{7,6},{8,9},{9,8},{10,11... | collective-permute-start | bytes 196616 | tf_op jit(solution)/shard_map/ppermute | solution.py:424
  26.1 5.3 %collective-permute-start.9 = (bf16[1,2,4,32,128]{4,3,2,1,0:T(8,128)(2,1)S(1)}, bf16[1,2,4,32,128]{4,3,2,1,0:T(8,128)(2,1)S(1)}, u32[]{:S(2)}, u32[]{:S(2)}) collective-permute-start(bf16[1,2,4,32,128]{4,3,2,1,0:T(8,128)(2,1)S(1)} %bitcast.15), channel_id=1, source_target_pairs={{0,16},{4,20},{8,24},{12,28},{16,0},{20,4},{24,8},{28,12},{1,17},{... | collective-permute-start | bytes 196616 | tf_op jit(solution)/shard_map/ppermute | solution.py:424
  31.5 3.6 %collective-permute-start.13 = (bf16[8,2,4,32,128]{4,3,2,1,0:T(8,128)(2,1)S(1)}, bf16[8,2,4,32,128]{4,3,2,1,0:T(8,128)(2,1)S(1)}, u32[]{:S(2)}, u32[]{:S(2)}) collective-permute-start(bf16[8,2,4,32,128]{4,3,2,1,0:T(8,128)(2,1)S(1)} %pad_maximum_fusion), channel_id=1, source_target_pairs={{0,4},{4,0},{8,12},{12,8},{16,20},{20,16},{24,28},{28,24},{1,5},{5... | collective-permute-start | bytes 1572872 | tf_op jit(solution)/shard_map/ppermute | solution.py:424
  32.6 7.5 %collective-permute-start.15 = (bf16[3,2,4,32,128]{4,3,2,1,0:T(8,128)(2,1)S(1)}, bf16[3,2,4,32,128]{4,3,2,1,0:T(8,128)(2,1)S(1)}, u32[]{:S(2)}, u32[]{:S(2)}) collective-permute-start(bf16[3,2,4,32,128]{4,3,2,1,0:T(8,128)(2,1)S(1)} %pad_maximum_fusion.4), channel_id=1, source_target_pairs={{0,16},{4,20},{8,24},{12,28},{16,0},{20,4},{24,8},{28,12},{1,17},{... | collective-permute-start | bytes 589832 | tf_op jit(solution)/shard_map/ppermute | solution.py:424
  33.8 6.3 %collective-permute-start.14 = (bf16[3,2,4,32,128]{4,3,2,1,0:T(8,128)(2,1)S(1)}, bf16[3,2,4,32,128]{4,3,2,1,0:T(8,128)(2,1)S(1)}, u32[]{:S(2)}, u32[]{:S(2)}) collective-permute-start(bf16[3,2,4,32,128]{4,3,2,1,0:T(8,128)(2,1)S(1)} %pad_maximum_fusion.4), channel_id=1, source_target_pairs={{0,8},{4,12},{8,0},{12,4},{16,24},{20,28},{24,16},{28,20},{1,9},{5... | collective-permute-start | bytes 589832 | tf_op jit(solution)/shard_map/ppermute | solution.py:424
  40.2 5.1 %collective-permute-start.18 = (bf16[4,2,4,32,128]{4,3,2,1,0:T(8,128)(2,1)S(1)}, bf16[4,2,4,32,128]{4,3,2,1,0:T(8,128)(2,1)S(1)}, u32[]{:S(2)}, u32[]{:S(2)}) collective-permute-start(bf16[4,2,4,32,128]{4,3,2,1,0:T(8,128)(2,1)S(1)} %pad_maximum_fusion.2.rest_0_.rest_2_), channel_id=1, source_target_pairs={{0,4},{4,0},{8,12},{12,8},{16,20},{20,16},{24,28},{28,24},{1,5},{5... | collective-permute-start | bytes 786440 | tf_op jit(solution)/shard_map/ppermute | solution.py:424
  41.3 4.0 %collective-permute-start.19 = (bf16[4,2,4,32,128]{4,3,2,1,0:T(8,128)(2,1)S(1)}, bf16[4,2,4,32,128]{4,3,2,1,0:T(8,128)(2,1)S(1)}, u32[]{:S(2)}, u32[]{:S(2)}) collective-permute-start(bf16[4,2,4,32,128]{4,3,2,1,0:T(8,128)(2,1)S(1)} %constant_dynamic-update-slice_fusion.rest_1_.rest_4_), channel_id=1, source_target_pairs={{0,4},{4,0},{8,12},{12,8},{16,20},{20,16},{24,28},{28,24},{1,5},{5... | collective-permute-start | bytes 786440 | tf_op jit(solution)/shard_map/ppermute | solution.py:424
  41.4 5.7 %collective-permute-start.17 = (bf16[2,2,4,32,128]{4,3,2,1,0:T(8,128)(2,1)S(1)}, bf16[2,2,4,32,128]{4,3,2,1,0:T(8,128)(2,1)S(1)}, u32[]{:S(2)}, u32[]{:S(2)}) collective-permute-start(bf16[2,2,4,32,128]{4,3,2,1,0:T(8,128)(2,1)S(1)} %slice.17), channel_id=1, source_target_pairs={{0,16},{4,20},{8,24},{12,28},{16,0},{20,4},{24,8},{28,12},{1,17},{... | collective-permute-start | bytes 393224 | tf_op jit(solution)/shard_map/ppermute | solution.py:424
  41.7 5.4 %collective-permute-start.16 = (bf16[2,2,4,32,128]{4,3,2,1,0:T(8,128)(2,1)S(1)}, bf16[2,2,4,32,128]{4,3,2,1,0:T(8,128)(2,1)S(1)}, u32[]{:S(2)}, u32[]{:S(2)}) collective-permute-start(bf16[2,2,4,32,128]{4,3,2,1,0:T(8,128)(2,1)S(1)} %slice.20), channel_id=1, source_target_pairs={{0,8},{4,12},{8,0},{12,4},{16,24},{20,28},{24,16},{28,20},{1,9},{5... | collective-permute-start | bytes 393224 | tf_op jit(solution)/shard_map/ppermute | solution.py:424
  47.1 2.7 %collective-permute-start.20 = (bf16[4,2,4,32,128]{4,3,2,1,0:T(8,128)(2,1)S(1)}, bf16[4,2,4,32,128]{4,3,2,1,0:T(8,128)(2,1)S(1)}, u32[]{:S(2)}, u32[]{:S(2)}) collective-permute-start(bf16[4,2,4,32,128]{4,3,2,1,0:T(8,128)(2,1)S(1)} %constant_dynamic-update-slice_fusion.2.rest_6_), channel_id=1, source_target_pairs={{0,4},{4,0},{8,12},{12,8},{16,20},{20,16},{24,28},{28,24},{1,5},{5... | collective-permute-start | bytes 786440 | tf_op jit(solution)/shard_map/ppermute | solution.py:424
